TPU v7x, 256 devices: a whole 4x4x8 slice. The times are simulated.
256 devices in a mesh: rel: 16 (over x, y), node: 16 (over z, core).
Axes of the slice: x: 4, y: 4, z: 8, core: 2. Of those that a mesh axis runs over, the one named last changes fastest.
Arguments:
- out_adjoint: bfloat16 [16, 1024, 512], P('node', 'rel'), may hold values from -6 to 6
- layer_input: bfloat16 [16, 1024, 512], P('node'), may hold values from -0.15625 to 0.15625
- rel_weights: bfloat16 [32, 512, 512], P('rel'), may hold values from -0.25 to 0.25
- self_weight: bfloat16 [512, 512], replicated, may hold values from -0.25 to 0.25
- tile_values: bfloat16 [16, 1024, 128, 128], P('rel', 'node'), may hold values from 0 to 0.039794922
- tile_rel: int32 [16, 1024], P('rel', 'node'), may hold values from 0 to 1
- tile_target: int32 [16, 1024], P('rel', 'node'), may hold values from 0 to 7
- tile_src: int32 [16, 1024], P('rel', 'node'), may hold values from 0 to 7
- tile_dest: int32 [16, 1024, 1], P('rel', 'node'), may hold values from 0 to 15; in each aligned block of 64 rows (0 to 63, 64 to 127, ..., all dimensions but the last counted through in order) at most 8 rows name the same one
Outputs:
- rel_weight_grad: float32 [32, 512, 512], P('rel', 'node')
- d_source: bfloat16 [16, 1024, 512], P('node', 'rel')
Inputs may be any that keep to these rules, and one draw needn't show every extreme that they name: `tile_dest`: among the 64 tiles of one device, at most 8 name the same node shard, and some node shard is named by exactly 8 of them.
All inputs are finite; a program needn't handle non-finite values.
Results may differ from a plain program's by a relative error of at most 0.0056.
Values may be sent and summed in bfloat16 or wider, within the bound.
A program may use at most 128 MiB of HBM per device.

v0:
```python
import jax
import jax.numpy as jnp
from jax import lax
from jax.sharding import PartitionSpec as P


def on_device(
    out_adjoint,
    layer_input,
    rel_weights,
    self_weight,
    tile_values,
    tile_rel,
    tile_target,
    tile_src,
    tile_dest,
):
    shard_count = lax.axis_size("node")
    tile_edge = tile_values.shape[-1]
    row_count = layer_input.shape[1]
    feature = layer_input.shape[2]
    blocks = row_count // tile_edge
    relations = rel_weights.shape[0]
    tile_count = tile_values.shape[1]
    capacity = 2 * tile_count // shard_count
    slot_count = shard_count * capacity
    adjoint = lax.all_gather(out_adjoint, "rel", axis=1, tiled=True)[0]
    owners = tile_dest[0, :, 0]
    relation = tile_rel[0]
    target = tile_target[0]
    source = tile_src[0]
    shared = owners[:, None] == owners[None, :]
    indices = jnp.arange(tile_count)
    earlier = indices[None, :] < indices[:, None]
    position = jnp.sum(jnp.logical_and(shared, earlier).astype(jnp.int32), axis=1)
    slot_of = owners * capacity + position
    placed = jnp.arange(slot_count)[:, None] == slot_of[None, :]
    placing = placed.astype(jnp.bfloat16)
    group_rows = lax.all_gather(adjoint[None], "node", axis=0, tiled=True)
    packed = relation * (blocks * blocks) + target * blocks + source
    outgoing = jnp.dot(
        placing,
        tile_values[0].reshape(tile_count, tile_edge * tile_edge),
        preferred_element_type=jnp.float32,
    )
    outgoing = outgoing.astype(jnp.bfloat16).reshape(shard_count, capacity, tile_edge, tile_edge)
    packed_slots = jnp.sum(jnp.where(placed, packed[None, :], 0), axis=1).reshape(
        shard_count, capacity
    )
    got_tiles, got_packed = (
        lax.all_to_all(outgoing, "node", split_axis=0, concat_axis=0, tiled=True),
        lax.all_to_all(packed_slots, "node", split_axis=0, concat_axis=0, tiled=True),
    )
    got_packed = got_packed.reshape(slot_count)
    got_target = got_packed // blocks % blocks
    bucket = got_packed // (blocks * blocks) * blocks + got_packed % blocks
    sender = jnp.arange(slot_count) // capacity
    chosen = jnp.take(
        group_rows.reshape(shard_count * blocks, tile_edge, feature),
        sender * blocks + got_target,
        axis=0,
    )
    partial_value = jnp.einsum(
        "sij,sid->sjd",
        got_tiles.reshape(slot_count, tile_edge, tile_edge),
        chosen,
        preferred_element_type=jnp.float32,
    )
    partial_value = partial_value.astype(jnp.bfloat16)
    onehot = (bucket[:, None] == jnp.arange(relations * blocks)[None, :]).astype(jnp.bfloat16)
    summed = jnp.einsum(
        "sk,sx->kx",
        onehot,
        partial_value.reshape(slot_count, tile_edge * feature),
        preferred_element_type=jnp.float32,
    )
    aggregated = summed.reshape(relations, row_count, feature).astype(jnp.bfloat16)
    weight_terms = jnp.einsum(
        "vi,rvj->rij", layer_input[0], aggregated, preferred_element_type=jnp.float32
    )
    rel_weight_grad = lax.psum_scatter(weight_terms, "node", scatter_dimension=1, tiled=True)
    own_rows = lax.psum_scatter(
        jnp.einsum("rvj,rij->vi", aggregated, rel_weights, preferred_element_type=jnp.float32),
        "rel",
        scatter_dimension=0,
        tiled=True,
    )
    self_term = jnp.einsum(
        "vj,ij->vi", out_adjoint[0], self_weight, preferred_element_type=jnp.float32
    )
    d_source = (own_rows + self_term).astype(jnp.bfloat16)[None]
    return (rel_weight_grad, d_source)


def solution(mesh):
    return jax.shard_map(
        on_device,
        mesh=mesh,
        in_specs=(
            P("node", "rel", None),
            P("node", None, None),
            P("rel", None, None),
            P(),
            P("rel", "node", None, None),
            P("rel", "node"),
            P("rel", "node"),
            P("rel", "node"),
            P("rel", "node", None),
        ),
        out_specs=(P("rel", "node", None), P("node", "rel", None)),
        check_vma=False,
    )
```

profile of v0, /device:TPU:1, one launch (start us, length us, event | category | flops | bytes accessed | tf_op | source)
XLA Modules:
  0.0 510.7 jit_solution(1792230578648732150)
XLA Ops:
  7.2 0.7 all-gather.3.cloned.1.call-update
  8.0 52.6 %all-gather.3.cloned.1.call-done = bf16[1,1024,512]{2,1,0:T(8,128)(2,1)} async-done(((bf16[1,64,512]{2,1,0:T(8,128)(2,1)}), bf16[1,1024,512]{2,1,0:T(8,128)(2,1)}) %all-gather.3.cloned.1.call-update) | async-done | bytes 1048592 | tf_op jit(solution)/shard_map/all_gather | solution.py:27
  60.6 0.9 convert_reduce_fusion
  61.5 0.7 multiply_add_fusion
  62.2 0.7 add_bitcast_fusion
  62.9 0.1 select_reduce_fusion
  63.0 0.7 all_to_all.9
  63.7 9.1 %all-to-all-start = ((s32[16,1,8]{2,1,0:T(1,128)}), s32[16,1,8]{2,1,0:T(1,128)S(1)}, u32[]{:S(2)}, u32[]{:S(2)}) async-start(s32[16,1,8]{2,1,0:T(1,128)} %bitcast.2), calls=%async_computation | async-start | bytes 16384 | tf_op jit(solution)/shard_map/all_to_all | solution.py:52
  72.8 5.2 %fusion.7 = bf16[16,8,128,128]{3,1,2,0:T(8,128)(2,1)} fusion(bf16[8,8,128,128]{3,2,1,0:T(8,128)(2,1)} %bitcast.43, s32[64]{0:T(128)S(1)} %multiply_add_fusion), kind=kOutput, calls=%fused_computation.8 | convolution fusion | flops 270540800 | bytes 6291712 | tf_op jit(solution)/shard_map/dot_general | solution.py:41
  78.0 1.9 all-to-all-done
  79.8 5.4 %all-to-all-start.1 = ((bf16[16,8,128,128]{3,1,2,0:T(8,128)(2,1)}), bf16[16,8,128,128]{3,1,2,0:T(8,128)(2,1)}, u32[]{:S(2)}, u32[]{:S(2)}) async-start(bf16[16,8,128,128]{3,1,2,0:T(8,128)(2,1)} %fusion.7), calls=%async_computation.1 | async-start | bytes 8388608 | tf_op jit(solution)/shard_map/all_to_all | solution.py:51
  85.2 0.5 broadcast.300
  85.8 0.7 reduce.5
  86.4 0.1 reshape.241
  86.5 0.1 reshape.245
  86.7 136.6 %all-to-all-done.1 = bf16[16,8,128,128]{3,1,2,0:T(8,128)(2,1)} async-done(((bf16[16,8,128,128]{3,1,2,0:T(8,128)(2,1)}), bf16[16,8,128,128]{3,1,2,0:T(8,128)(2,1)}, u32[]{:S(2)}, u32[]{:S(2)}) %all-to-all-start.1) | async-done | bytes 4194336 | tf_op jit(solution)/shard_map/all_to_all | solution.py:51
  223.3 6.9 %copy.23 = bf16[16,8,128,128]{2,3,1,0:T(8,128)(2,1)} copy(bf16[16,8,128,128]{3,1,2,0:T(8,128)(2,1)} %all-to-all-done.1) | data formatting | bytes 8388608 | tf_op jit(solution)/shard_map/all_to_all | solution.py:51
  230.1 18.8 %all-gather.5.cloned.1.call-done = bf16[16,1024,512]{2,1,0:T(8,128)(2,1)} async-done(((bf16[1,1024,512]{2,1,0:T(8,128)(2,1)}), bf16[16,1024,512]{2,1,0:T(8,128)(2,1)}) %all-gather.5.cloned.1.call-update) | async-done | bytes 16777232 | tf_op jit(solution)/shard_map/all_gather | solution.py:39
  248.9 14.1 %gather_fusion = bf16[128,128,512]{2,1,0:T(8,128)(2,1)} fusion(bf16[128,128,512]{2,1,0:T(8,128)(2,1)} %bitcast.42, s32[1024]{0:T(1024)S(1)} %pad_clamp_fusion), kind=kCustom, calls=%fused_computation | custom fusion | bytes 33554944 | tf_op jit(solution)/shard_map/jit(_take)/gather | solution.py:58
  263.0 15.7 %fusion.3 = bf16[128,128,512]{2,1,0:T(8,128)(2,1)} fusion(bf16[128,128,128]{1,2,0:T(8,128)(2,1)} %bitcast.41, bf16[128,128,512]{2,1,0:T(8,128)(2,1)} %gather_fusion, pred[128]{0:T(512)(128)(4,1)S(1)} %compare_and_fusion), kind=kOutput, calls=%fused_computation.6 | convolution fusion | flops 2164260864 | bytes 37748864 | tf_op jit(solution)/shard_map/sij,sid->sjd/dot_general | solution.py:63
  278.7 15.8 %copy.29 = bf16[16,8,128,512]{3,1,2,0:T(8,128)(2,1)S(1)} copy(bf16[16,8,128,512]{3,2,1,0:T(8,128)(2,1)} %bitcast.39) | data formatting | bytes 33554432
  294.6 2.6 convolution_convert_fusion
  297.2 2.0 convert_element_type.25
  299.2 4.2 convolution_bitcast_fusion.1
  303.4 4.2 copy.25
  307.8 3.8 convolution_bitcast_fusion
  311.6 0.6 dynamic-slice
  312.9 107.8 %all-reduce.3.cloned.1.call-done = f32[2,512,512]{2,0,1:T(2,128)} async-done(((f32[2,512,512]{2,0,1:T(2,128)}), f32[2,512,512]{2,0,1:T(2,128)}) %all-reduce.3.cloned.1.call-update) | async-done | bytes 2097168
  420.6 0.9 constant_dynamic-slice_fusion
  421.5 0.7 copy.26
  422.2 80.0 %reduce-scatter.2.cloned.1.call-done = f32[64,512]{1,0:T(8,128)} async-done(((f32[1024,512]{1,0:T(8,128)}), f32[64,512]{1,0:T(8,128)}) %reduce-scatter.2.cloned.1.call-update) | async-done | bytes 131088 | tf_op jit(solution)/shard_map/reduce_scatter | solution.py:82
  502.2 2.0 fusion.11
  (19 shorter events, 0.3 us)
Async XLA Ops:
  7.2 292.1 %copy-start = (bf16[1,1024,512]{2,1,0:T(8,128)(2,1)S(1)}, bf16[1,1024,512]{2,1,0:T(8,128)(2,1)}, u32[]{:S(2)}) copy-start(bf16[1,1024,512]{2,1,0:T(8,128)(2,1)} %param.10) | copy-start | bytes 3145732
  7.2 53.4 %all-gather.3.cloned.1.call-start = ((), (), s32[]{:S(2)}) async-start(), calls=%async_computation.3 | async-start | bytes 1114112 | tf_op jit(solution)/shard_map/all_gather | solution.py:27
  7.9 241.0 %all-gather.5.cloned.1.call-start = ((), (), s32[]{:S(2)}) async-start(), calls=%async_computation.4 | async-start | bytes 17825792 | tf_op jit(solution)/shard_map/all_gather | solution.py:39
  63.7 16.2 %all-to-all-start = ((s32[16,1,8]{2,1,0:T(1,128)}), s32[16,1,8]{2,1,0:T(1,128)S(1)}, u32[]{:S(2)}, u32[]{:S(2)}) async-start(s32[16,1,8]{2,1,0:T(1,128)} %bitcast.2), calls=%async_computation | async-start | bytes 16384 | tf_op jit(solution)/shard_map/all_to_all | solution.py:52
  79.8 143.5 %all-to-all-start.1 = ((bf16[16,8,128,128]{3,1,2,0:T(8,128)(2,1)}), bf16[16,8,128,128]{3,1,2,0:T(8,128)(2,1)}, u32[]{:S(2)}, u32[]{:S(2)}) async-start(bf16[16,8,128,128]{3,1,2,0:T(8,128)(2,1)} %fusion.7), calls=%async_computation.1 | async-start | bytes 8388608 | tf_op jit(solution)/shard_map/all_to_all | solution.py:51
  85.2 335.4 %all-reduce.3.cloned.1.call-start = ((), (), s32[]{:S(2)}) async-start(), calls=%async_computation.6 | async-start | bytes 4194304
  303.4 4.4 copy-start.1
  307.7 3.9 copy-start.3
  307.7 194.5 %copy-start.2 = (bf16[1,64,512]{2,1,0:T(8,128)(2,1)S(1)}, bf16[1,64,512]{2,1,0:T(8,128)(2,1)}, u32[]{:S(2)}) copy-start(bf16[1,64,512]{2,1,0:T(8,128)(2,1)} %param.9) | copy-start | bytes 196612
  307.7 194.5 %reduce-scatter.2.cloned.1.call-start = ((), (), s32[]{:S(2)}) async-start(), calls=%async_computation.5 | async-start | bytes 2228224 | tf_op jit(solution)/shard_map/reduce_scatter | solution.py:82
Sparse Core Ops, SparseCore 0:
  10.4 50.0 all-gather.2
  62.4 186.4 all-gather.4
  307.8 112.7 all-reduce.2
  424.0 78.1 reduce-scatter.1
where the time goes:
time: 512 us; the launch traced here: 511 us
  waiting for transfers between devices  398 us (78%)
  local copies, waits for them, and re-layouts  46.6 us (9%)
  matrix products  33.5 us (7%)
  starting transfers between devices  14.7 us (3%)
  between operations  14.5 us (3%)
    all_to_all x1, waiting for transfers between devices, on_device(): lax.all_to_all(outgoing, 'node', split_axis=0, concat_axis=0, tiled=True)  137 us
    unnamed x5, waiting for transfers between devices  108 us
    reduce_scatter x1, waiting for transfers between devices, on_device(): lax.psum_scatter(jnp.einsum('rvj,rij->vi', aggregated, rel_weights, prefe...  80 us
    all_gather x1, waiting for transfers between devices, on_device(): adjoint = lax.all_gather(out_adjoint, 'rel', axis=1, tiled=True)[0]  52.6 us
    all_gather x1, waiting for transfers between devices, on_device(): group_rows = lax.all_gather(adjoint[None], 'node', axis=0, tiled=True)  18.8 us
    unnamed x12, local copies, waits for them, and re-layouts  18.1 us
    dot_general x1, matrix products, on_device(): jnp.einsum('sij,sid->sjd', got_tiles.reshape(slot_count, tile_edge, tile_...  15.7 us
    gather x1, local copies, waits for them, and re-layouts, on_device(): jnp.take(group_rows.reshape(shard_count * blocks, tile_edge, feature), se...  14.1 us
  transfers between devices with their start and end apart: 6, of which 6 were waited for; matrix products, arithmetic and copies ran while one was open for 4% of the time, Pallas kernels for 0%

commit v1 on v0

v1 whole, which is shorter than its diff:
```python
import jax
import jax.numpy as jnp
from jax import lax
from jax.experimental import pallas as pl
from jax.experimental.pallas import tpu as pltpu
from jax.sharding import PartitionSpec as P

MESH = pl.DeviceIdType.MESH
ANY = pl.BlockSpec(memory_space=pl.ANY)
VMEM = pl.BlockSpec(memory_space=pltpu.VMEM)
SMEM = pl.BlockSpec(memory_space=pltpu.SMEM)

SIDE = 4
NODES = 16
ROWS = 64
QUARTER = 128
TILES = 64
EDGE = 128
FEATURE = 512
BLOCKS = 8
CHUNK = 16


def place():
    rel, node = lax.axis_index("rel"), lax.axis_index("node")
    return (
        lax.div(rel, SIDE),
        lax.rem(rel, SIDE),
        lax.div(node, 2),
        lax.rem(node, 2),
        rel,
        node,
    )


def quarter_of(node):
    return lax.rem(lax.div(node, 2), 2) * 2 + lax.rem(node, 2)


def greet(x, y, rel, node):
    barrier = pltpu.get_barrier_semaphore()

    def call(there_rel, there_node):
        pl.semaphore_signal(
            barrier, inc=1, device_id=(there_rel, there_node), device_id_type=MESH
        )

    for k in range(1, SIDE):
        call(lax.rem(x + k, SIDE) * SIDE + y, node)
        call(x * SIDE + lax.rem(y + k, SIDE), node)
    for k in range(1, NODES):
        call(rel, lax.rem(node + k, NODES))
    pl.semaphore_wait(barrier, 2 * (SIDE - 1) + NODES - 1)


def push(src, dst, send, recv, there):
    copy = pltpu.make_async_remote_copy(
        src_ref=src,
        dst_ref=dst,
        send_sem=send,
        recv_sem=recv,
        device_id=there,
        device_id_type=MESH,
    )
    copy.start()
    return copy


def gather_kernel(
    adj,
    layer,
    tiles,
    meta,
    t_all,
    a_all,
    x_all,
    m_all,
    local_sem,
    a_send,
    a_recv,
    x_send,
    x_recv,
    z_send,
    z_recv,
    t_send,
    t_recv,
    s_send,
    s_recv,
    m_send,
    m_recv,
):
    x, y, z, c, rel, node = place()
    half = ROWS // 2
    own = 1 + c
    sibling = (rel, z * 2 + (1 - c))
    beside = lax.rem(z + 7 + 2 * c, 8)
    away = 3 * (1 - c)
    quarter = quarter_of(node)

    def x_peer(k):
        return (lax.rem(x + k, SIDE) * SIDE + y, node)

    def y_peer(k):
        return (x * SIDE + lax.rem(y + k, SIDE), node)

    greet(x, y, rel, node)

    a_first = []
    for k in range(1, SIDE):
        a_first.append(
            push(
                adj.at[pl.ds(0, half)],
                a_all.at[own, x, y, pl.ds(0, half)],
                a_send.at[0, k - 1],
                a_recv.at[0, k - 1],
                x_peer(k),
            )
        )
        a_first.append(
            push(
                adj.at[pl.ds(half, half)],
                a_all.at[own, x, y, pl.ds(half, half)],
                a_send.at[1, k - 1],
                a_recv.at[1, k - 1],
                y_peer(k),
            )
        )
    a_own = pltpu.make_async_copy(adj, a_all.at[own, x, y], local_sem.at[0])
    a_own.start()

    z_copies = []
    for k in range(1, NODES):
        there = lax.rem(node + k, NODES)
        column = pl.multiple_of(quarter_of(there) * QUARTER, QUARTER)
        z_copies.append(
            push(
                layer.at[pl.ds(rel * ROWS, ROWS), pl.ds(column, QUARTER)],
                x_all.at[node, x, y],
                z_send.at[k - 1],
                z_recv.at[k - 1],
                (rel, there),
            )
        )
    x_own = pltpu.make_async_copy(
        layer.at[
            pl.ds(rel * ROWS, ROWS),
            pl.ds(pl.multiple_of(quarter * QUARTER, QUARTER), QUARTER),
        ],
        x_all.at[node, x, y],
        local_sem.at[1],
    )
    x_own.start()

    m_copies = [push(meta, m_all.at[own], m_send.at[0], m_recv.at[0], sibling)]
    m_own = pltpu.make_async_copy(meta, m_all.at[own], local_sem.at[2])
    m_own.start()
    t_own = pltpu.make_async_copy(tiles, t_all.at[own], local_sem.at[3])
    t_own.start()
    t_far = []
    for h in range(2):
        there = (rel, beside * 2 + h)
        m_copies.append(
            push(meta, m_all.at[away], m_send.at[1 + h], m_recv.at[1 + c], there)
        )
        part = pl.ds(h * (TILES // 2), TILES // 2)
        t_far.append(
            push(
                tiles.at[part],
                t_all.at[away, part],
                t_send.at[h],
                t_recv.at[c],
                there,
            )
        )
    t_near = push(tiles, t_all.at[own], s_send.at[0], s_recv.at[0], sibling)

    def arrival(ref, sem):
        pltpu.make_async_copy(ref, ref, sem).wait()

    a_own.wait()
    for copy in a_first:
        copy.wait()
    a_second = []
    for k in range(1, SIDE):
        mine = a_all.at[own, :, y, pl.ds(0, half)]
        a_second.append(
            push(mine, mine, a_send.at[2, k - 1], a_recv.at[2, k - 1], y_peer(k))
        )
        mine = a_all.at[own, x, :, pl.ds(half, half)]
        a_second.append(
            push(mine, mine, a_send.at[3, k - 1], a_recv.at[3, k - 1], x_peer(k))
        )

    x_own.wait()
    for copy in z_copies:
        copy.wait()
    x_first = []
    for k in range(1, SIDE):
        mine = x_all.at[pl.ds(0, 8), x, y]
        x_first.append(
            push(mine, mine, x_send.at[0, k - 1], x_recv.at[0, k - 1], x_peer(k))
        )
        mine = x_all.at[pl.ds(8, 8), x, y]
        x_first.append(
            push(mine, mine, x_send.at[1, k - 1], x_recv.at[1, k - 1], y_peer(k))
        )

    for copy in a_second:
        copy.wait()
    a_far = []
    for h in range(2):
        part = pl.ds(2 * h, 2)
        a_far.append(
            push(
                a_all.at[own, part],
                a_all.at[away, part],
                t_send.at[2 + h],
                t_recv.at[2 + c],
                (rel, beside * 2 + h),
            )
        )
    a_near = push(
        a_all.at[own], a_all.at[own], s_send.at[1], s_recv.at[1], sibling
    )

    for copy in x_first:
        copy.wait()
    x_second = []
    for k in range(1, SIDE):
        mine = x_all.at[pl.ds(0, 8), :, y]
        x_second.append(
            push(mine, mine, x_send.at[2, k - 1], x_recv.at[2, k - 1], y_peer(k))
        )
        mine = x_all.at[pl.ds(8, 8), x]
        x_second.append(
            push(mine, mine, x_send.at[3, k - 1], x_recv.at[3, k - 1], x_peer(k))
        )

    onward = []
    mine = pl.ds(c * (TILES // 2), TILES // 2)
    rows = pl.ds(2 * c, 2)
    for sender, slot in ((0, 3), (1, 0)):
        arrival(t_all.at[slot, mine], t_recv.at[sender])
        onward.append(
            push(
                t_all.at[slot, mine],
                t_all.at[slot, mine],
                s_send.at[2 + sender],
                s_recv.at[2 + sender],
                sibling,
            )
        )
    for sender, slot in ((0, 3), (1, 0)):
        arrival(a_all.at[slot, rows], t_recv.at[2 + sender])
        onward.append(
            push(
                a_all.at[slot, rows],
                a_all.at[slot, rows],
                s_send.at[4 + sender],
                s_recv.at[4 + sender],
                sibling,
            )
        )

    for copy in t_far + a_far:
        copy.wait_send()
    other = 2 - c
    t_near.wait_send()
    a_near.wait_send()
    arrival(t_all.at[other], s_recv.at[0])
    arrival(a_all.at[other], s_recv.at[1])
    theirs = pl.ds((1 - c) * (TILES // 2), TILES // 2)
    their_rows = pl.ds(2 * (1 - c), 2)
    for copy in onward:
        copy.wait_send()
    for sender, slot in ((0, 3), (1, 0)):
        arrival(t_all.at[slot, theirs], s_recv.at[2 + sender])
        arrival(a_all.at[slot, their_rows], s_recv.at[4 + sender])
    for copy in m_copies:
        copy.wait_send()
    arrival(m_all.at[other], m_recv.at[0])
    arrival(m_all.at[3], m_recv.at[1])
    arrival(m_all.at[0], m_recv.at[2])
    m_own.wait()
    t_own.wait()
    for copy in x_second:
        copy.wait()


def gather(adj, layer, tiles, meta):
    dma = pltpu.SemaphoreType.DMA
    return pl.pallas_call(
        gather_kernel,
        out_shape=(
            jax.ShapeDtypeStruct((4, TILES, EDGE, EDGE), jnp.bfloat16),
            jax.ShapeDtypeStruct((4, SIDE, SIDE, ROWS, FEATURE), jnp.bfloat16),
            jax.ShapeDtypeStruct((NODES, SIDE, SIDE, ROWS, QUARTER), jnp.bfloat16),
            jax.ShapeDtypeStruct((4, 8, 128), jnp.int32),
        ),
        in_specs=[ANY] * 4,
        out_specs=(ANY,) * 4,
        scratch_shapes=[
            dma((4,)),
            dma((4, 3)),
            dma((4, 3)),
            dma((4, 3)),
            dma((4, 3)),
            dma((15,)),
            dma((15,)),
            dma((4,)),
            dma((4,)),
            dma((6,)),
            dma((6,)),
            dma((3,)),
            dma((3,)),
        ],
        compiler_params=pltpu.CompilerParams(collective_id=0, has_side_effects=True),
        cost_estimate=pl.CostEstimate(
            flops=0, bytes_accessed=32 << 20, transcendentals=0
        ),
        name="gather_rows_and_tiles",
    )(adj, layer, tiles, meta)


def local_kernel(meta, tiles, a_rows, x_rows, weights, d_out, g_out, aw, d_sum, h_sum):
    step = pl.program_id(0)
    last = pl.num_programs(0) - 1
    quarter = quarter_of(lax.axis_index("node"))
    blocks = 4 * BLOCKS

    @pl.when(step == 0)
    def _():
        d_sum[...] = jnp.zeros_like(d_sum)
        h_sum[...] = jnp.zeros_like(h_sum)
        column = pl.multiple_of(quarter * QUARTER, QUARTER)

        def one(b, carry):
            rows = a_rows[b]
            for r in range(2):
                aw[r, b] = lax.dot_general(
                    weights[r, pl.ds(column, QUARTER), :],
                    rows,
                    (((1,), (1,)), ((), ())),
                    preferred_element_type=jnp.float32,
                ).astype(jnp.bfloat16)
            return carry

        lax.fori_loop(0, blocks, one, 0)

    slot = lax.div(step * CHUNK, TILES)
    first = lax.rem(step * CHUNK, TILES)
    for k in range(CHUNK):
        code = meta[slot, 0, first + k]
        target = slot * BLOCKS + lax.rem(code, BLOCKS)
        relation = lax.rem(lax.div(code, BLOCKS), 2)
        bucket = lax.div(code, 2 * BLOCKS)
        tile = tiles[k]
        d_sum[bucket] += jnp.dot(
            aw[relation, target], tile, preferred_element_type=jnp.float32
        )
        h_sum[relation, target] += jnp.dot(
            tile, x_rows[bucket], preferred_element_type=jnp.float32
        )

    @pl.when(step == last)
    def _():
        def turn(b, carry):
            d_out[b] = d_sum[b].T.astype(jnp.bfloat16)
            return carry

        lax.fori_loop(0, NODES * BLOCKS, turn, 0)
        for r in range(2):

            def add(b, total):
                turned = h_sum[r, b].T.astype(jnp.bfloat16)
                return total + jnp.dot(
                    turned, a_rows[b], preferred_element_type=jnp.float32
                )

            g_out[r] = lax.fori_loop(
                0, blocks, add, jnp.zeros((QUARTER, FEATURE), jnp.float32)
            )


def local(meta, tiles, a_rows, x_rows, weights):
    buckets = NODES * BLOCKS
    steps = 4 * TILES // CHUNK
    return pl.pallas_call(
        local_kernel,
        grid=(steps,),
        out_shape=(
            jax.ShapeDtypeStruct((buckets, EDGE, QUARTER), jnp.bfloat16),
            jax.ShapeDtypeStruct((2, QUARTER, FEATURE), jnp.float32),
        ),
        in_specs=[
            SMEM,
            pl.BlockSpec((CHUNK, EDGE, EDGE), lambda s: (s, 0, 0)),
            VMEM,
            VMEM,
            VMEM,
        ],
        out_specs=(VMEM, VMEM),
        scratch_shapes=[
            pltpu.VMEM((2, 4 * BLOCKS, QUARTER, EDGE), jnp.bfloat16),
            pltpu.VMEM((buckets, QUARTER, EDGE), jnp.float32),
            pltpu.VMEM((2, 4 * BLOCKS, EDGE, QUARTER), jnp.float32),
        ],
        compiler_params=pltpu.CompilerParams(
            vmem_limit_bytes=56 << 20, dimension_semantics=("arbitrary",)
        ),
        name="tile_products",
    )(meta, tiles, a_rows, x_rows, weights)


def reduce_kernel(
    d_part,
    g_part,
    adj,
    self_weight,
    g_out,
    d_out,
    own_a,
    own_b,
    got_a,
    got_b,
    sum_a,
    sum_b,
    next_a,
    next_b,
    total,
    got_z,
    got_g,
    own_term,
    local_sem,
    a_send,
    a_recv,
    z_send,
    z_recv,
    g_send,
    g_recv,
):
    x, y, z, c, rel, node = place()
    quarter = quarter_of(node)
    half = NODES // 2

    def x_peer(k):
        return (lax.rem(x + k, SIDE) * SIDE + y, node)

    def y_peer(k):
        return (x * SIDE + lax.rem(y + k, SIDE), node)

    greet(x, y, rel, node)

    first = []
    for k in range(1, SIDE):
        first.append(
            push(
                d_part.at[pl.ds(0, half), lax.rem(x + k, SIDE)],
                got_a.at[k - 1],
                a_send.at[0, k - 1],
                a_recv.at[0, k - 1],
                x_peer(k),
            )
        )
        first.append(
            push(
                d_part.at[pl.ds(half, half), :, lax.rem(y + k, SIDE)],
                got_b.at[k - 1],
                a_send.at[1, k - 1],
                a_recv.at[1, k - 1],
                y_peer(k),
            )
        )
    mine_a = pltpu.make_async_copy(
        d_part.at[pl.ds(0, half), x], own_a, local_sem.at[0]
    )
    mine_a.start()
    mine_b = pltpu.make_async_copy(
        d_part.at[pl.ds(half, half), :, y], own_b, local_sem.at[1]
    )
    mine_b.start()

    sender = lax.div(z, 2)
    for m in range(4):
        owner = quarter * 4 + m
        rows = g_part.at[:, pl.ds(32 * m, 32), :]

        @pl.when(owner != node)
        def _():
            push(
                rows,
                got_g.at[sender],
                g_send.at[m],
                g_recv.at[sender],
                (rel, owner),
            )

        @pl.when(owner == node)
        def _():
            pltpu.make_async_copy(rows, got_g.at[sender], g_recv.at[sender]).start()

    own_term[...] = lax.dot_general(
        adj[...],
        self_weight[...],
        (((1,), (1,)), ((), ())),
        preferred_element_type=jnp.float32,
    )

    mine_a.wait()
    mine_b.wait()
    for copy in first:
        copy.wait()

    def f32(value):
        return value.astype(jnp.float32)

    def add_first(n, carry):
        for own, got, into in ((own_a, got_a, sum_a), (own_b, got_b, sum_b)):
            value = f32(own[n])
            for k in range(SIDE - 1):
                value = value + f32(got[k, n])
            into[n] = value.astype(jnp.bfloat16)
        return carry

    lax.fori_loop(0, half, add_first, 0)

    second = []
    for k in range(1, SIDE):
        second.append(
            push(
                sum_a.at[:, lax.rem(y + k, SIDE)],
                next_a.at[k - 1],
                a_send.at[2, k - 1],
                a_recv.at[2, k - 1],
                y_peer(k),
            )
        )
        second.append(
            push(
                sum_b.at[:, lax.rem(x + k, SIDE)],
                next_b.at[k - 1],
                a_send.at[3, k - 1],
                a_recv.at[3, k - 1],
                x_peer(k),
            )
        )

    for m in range(4):
        pltpu.make_async_copy(got_g.at[m], got_g.at[m], g_recv.at[m]).wait()
        owner = quarter * 4 + m
        rows = g_part.at[:, pl.ds(32 * m, 32), :]

        @pl.when(owner != node)
        def _():
            pltpu.make_async_remote_copy(
                src_ref=rows,
                dst_ref=got_g.at[sender],
                send_sem=g_send.at[m],
                recv_sem=g_recv.at[sender],
                device_id=(rel, owner),
                device_id_type=MESH,
            ).wait_send()

    g_out[...] = (got_g[0] + got_g[1]) + (got_g[2] + got_g[3])

    for copy in second:
        copy.wait()

    def add_second(n, carry):
        for own, at, got, base in (
            (sum_a, y, next_a, 0),
            (sum_b, x, next_b, half),
        ):
            value = f32(own[n, at])
            for k in range(SIDE - 1):
                value = value + f32(got[k, n])
            total[base + n] = value.astype(jnp.bfloat16)
        return carry

    lax.fori_loop(0, half, add_second, 0)

    z_copies = []
    for k in range(1, NODES):
        there = lax.rem(node + k, NODES)
        z_copies.append(
            push(
                total.at[there],
                got_z.at[node],
                z_send.at[k - 1],
                z_recv.at[k - 1],
                (rel, there),
            )
        )
    mine_z = pltpu.make_async_copy(total.at[node], got_z.at[node], local_sem.at[2])
    mine_z.start()
    mine_z.wait()
    for copy in z_copies:
        copy.wait()
    for q in range(4):
        columns = pl.ds(q * QUARTER, QUARTER)
        value = own_term[:, columns]
        for step in range(4):
            value = value + f32(got_z[(2 * step + q // 2) * 2 + q % 2])
        d_out[:, columns] = value.astype(jnp.bfloat16)


def reduce(d_part, g_part, adj, self_weight):
    dma = pltpu.SemaphoreType.DMA
    half = NODES // 2
    bf16 = jnp.bfloat16
    return pl.pallas_call(
        reduce_kernel,
        out_shape=(
            jax.ShapeDtypeStruct((2, 32, FEATURE), jnp.float32),
            jax.ShapeDtypeStruct((ROWS, FEATURE), bf16),
        ),
        in_specs=[ANY, ANY, VMEM, VMEM],
        out_specs=(VMEM, VMEM),
        scratch_shapes=[
            pltpu.VMEM((half, SIDE, ROWS, QUARTER), bf16),
            pltpu.VMEM((half, SIDE, ROWS, QUARTER), bf16),
            pltpu.VMEM((3, half, SIDE, ROWS, QUARTER), bf16),
            pltpu.VMEM((3, half, SIDE, ROWS, QUARTER), bf16),
            pltpu.VMEM((half, SIDE, ROWS, QUARTER), bf16),
            pltpu.VMEM((half, SIDE, ROWS, QUARTER), bf16),
            pltpu.VMEM((3, half, ROWS, QUARTER), bf16),
            pltpu.VMEM((3, half, ROWS, QUARTER), bf16),
            pltpu.VMEM((NODES, ROWS, QUARTER), bf16),
            pltpu.VMEM((NODES, ROWS, QUARTER), bf16),
            pltpu.VMEM((4, 2, 32, FEATURE), jnp.float32),
            pltpu.VMEM((ROWS, FEATURE), jnp.float32),
            dma((3,)),
            dma((4, 3)),
            dma((4, 3)),
            dma((15,)),
            dma((15,)),
            dma((4,)),
            dma((4,)),
        ],
        compiler_params=pltpu.CompilerParams(
            collective_id=1, has_side_effects=True, vmem_limit_bytes=32 << 20
        ),
        name="sum_terms",
    )(d_part, g_part, adj, self_weight)


def on_device(
    out_adjoint,
    layer_input,
    rel_weights,
    self_weight,
    tile_values,
    tile_rel,
    tile_target,
    tile_src,
    tile_dest,
):
    code = (
        (tile_dest[:, :, 0] * BLOCKS + tile_src) * 2 + tile_rel
    ) * BLOCKS + tile_target
    meta = jnp.pad(code, ((0, 7), (0, 128 - TILES)))
    adj = out_adjoint[0]
    tiles, a_rows, x_rows, codes = gather(adj, layer_input[0], tile_values[0], meta)
    d_part, g_part = local(
        codes,
        tiles.reshape(4 * TILES, EDGE, EDGE),
        a_rows.reshape(4 * BLOCKS, EDGE, FEATURE),
        x_rows.reshape(NODES * BLOCKS, EDGE, QUARTER),
        rel_weights,
    )
    rel_weight_grad, d_source = reduce(
        d_part.reshape(NODES, SIDE, SIDE, ROWS, QUARTER), g_part, adj, self_weight
    )
    return rel_weight_grad, d_source[None]


def solution(mesh):
    return jax.shard_map(
        on_device,
        mesh=mesh,
        in_specs=(
            P("node", "rel", None),
            P("node", None, None),
            P("rel", None, None),
            P(),
            P("rel", "node", None, None),
            P("rel", "node"),
            P("rel", "node"),
            P("rel", "node"),
            P("rel", "node", None),
        ),
        out_specs=(P("rel", "node", None), P("node", "rel", None)),
        check_vma=False,
    )
```

time: 512 us -> 186 us (0.36)
  waiting for transfers between devices: 398 us -> 0 us
  Pallas kernels: 0 us -> 179 us
  local copies, waits for them, and re-layouts: 46.6 us -> 5.12 us
  matrix products: 33.5 us -> 0 us
  starting transfers between devices: 14.7 us -> 0 us
  between operations: 14.5 us -> 0.68 us
    pallas_call x0 -> x3, Pallas kernels: none -> 179 us  [the longest x1 76.6 us: gather(): pl.pallas_call(gather_kernel, out_shape=(jax.ShapeDtypeStruct((4, TILES,...]
    all_to_all x2 -> x0, waiting for transfers between devices: 138 us -> none  [the longest x1 137 us: on_device(): lax.all_to_all(outgoing, 'node', split_axis=0, concat_axis=0, tiled=True)]
    unnamed x5 -> x0, waiting for transfers between devices: 108 us -> none
    reduce_scatter x1 -> x0, waiting for transfers between devices: 80 us -> none  [on_device(): lax.psum_scatter(jnp.einsum('rvj,rij->vi', aggregated, rel_weights, prefe...]
    all_gather x2 -> x0, waiting for transfers between devices: 71.4 us -> none  [the longest x1 52.6 us: on_device(): adjoint = lax.all_gather(out_adjoint, 'rel', axis=1, tiled=True)[0]]
    dot_general x6 -> x0, matrix products: 33.5 us -> none  [the longest x1 15.7 us: on_device(): jnp.einsum('sij,sid->sjd', got_tiles.reshape(slot_count, tile_edge, tile_...]
    all_to_all x2 -> x0, starting transfers between devices: 14.5 us -> none  [the longest x1 9.13 us: on_device(): lax.all_to_all(packed_slots, 'node', split_axis=0, concat_axis=0, tiled=T...]
    gather x1 -> x0, local copies, waits for them, and re-layouts: 14.1 us -> none  [on_device(): jnp.take(group_rows.reshape(shard_count * blocks, tile_edge, feature), se...]
  transfers between devices with their start and end apart: 6 -> 0, of which waited for: 6 -> 0; matrix products, arithmetic and copies ran while one was open for 4% -> 0% of each run, Pallas kernels for 0% -> 0%
where the time goes in v1:
time: 186 us
  Pallas kernels  179 us (96%)
  local copies, waits for them, and re-layouts  5.12 us (3%)
    pallas_call x1, Pallas kernels, gather(): pl.pallas_call(gather_kernel, out_shape=(jax.ShapeDtypeStruct((4, TILES,...  76.6 us
    pallas_call x1, Pallas kernels, local(): pl.pallas_call(local_kernel, grid=(steps,), out_shape=(jax.ShapeDtypeStru...  54.5 us
    pallas_call x1, Pallas kernels, reduce(): pl.pallas_call(reduce_kernel, out_shape=(jax.ShapeDtypeStruct((2, 32, FEA...  48.1 us
    unnamed x10, local copies, waits for them, and re-layouts  4.52 us

profile of v1, /device:TPU:1, one launch (start us, length us, event | category | flops | bytes accessed | tf_op | source)
XLA Modules:
  0.0 185.7 jit_solution(14476617690664518703)
XLA Ops:
  0.6 0.7 multiply_add_fusion
  1.3 0.6 pad.4.meta
  1.9 76.6 %gather_rows_and_tiles.1 = (bf16[4,64,128,128]{3,2,1,0:T(8,128)(2,1)}, bf16[4,4,4,64,512]{4,3,2,1,0:T(8,128)(2,1)}, bf16[16,4,4,64,128]{4,3,2,1,0:T(8,128)(2,1)}, s32[4,8,128]{2,1,0:T(8,128)}) custom-call(bf16[64,512]{1,0:T(8,128)(2,1)} %bitcast.17, bf16[1024,512]{1,0:T(8,128)(2,1)} %bitcast.24, bf16[64,128,128]{2,1,0:T(8,128)(2,1)} %bitcast.23, ...), custom_call_target="tpu_custom_call" | custom-call | bytes 33554432 | tf_op jit(solution)/shard_map/gather_rows_and_tiles/pallas_call | solution.py:292
  78.5 0.0 copy-start.1
  78.5 0.0 copy-start.3
  78.5 54.5 %tile_products.1 = (bf16[128,128,128]{2,1,0:T(8,128)(2,1)}, f32[2,128,512]{2,1,0:T(8,128)}) custom-call(s32[4,8,128]{2,1,0:T(8,128)} %get-tuple-element.10.meta, bf16[256,128,128]{2,1,0:T(8,128)(2,1)} %bitcast.20, bf16[32,128,512]{2,1,0:T(8,128)(2,1)} %bitcast.21, bf16[128,128,128]{2,1,0:T(8,128)(2,1)} %bitcast.22, bf16[2,512,512]{2,1,0:T(8,128)(2,1)} %weights.1), custom_call_target="tpu_custom_call" | custom-call | tf_op jit(solution)/shard_map/tile_products/pallas_call | solution.py:388
  133.0 0.0 copy-done.1
  133.0 0.0 copy-done.3
  133.0 0.0 copy-start
  133.0 2.2 %copy-done = bf16[128,128,128]{2,1,0:T(8,128)(2,1)S(1)} copy-done((bf16[128,128,128]{2,1,0:T(8,128)(2,1)S(1)}, bf16[128,128,128]{2,1,0:T(8,128)(2,1)}, u32[]{:S(2)}) %copy-start) | copy-done | bytes 4194328
  135.2 0.0 copy-start.2
  135.2 1.0 copy-done.2
  136.3 48.1 %sum_terms.1 = (f32[2,32,512]{2,1,0:T(8,128)S(1)}, bf16[64,512]{1,0:T(8,128)(2,1)S(1)}) custom-call(bf16[16,4,4,64,128]{4,3,2,1,0:T(8,128)(2,1)S(1)} %bitcast.16, f32[2,128,512]{2,1,0:T(8,128)S(1)} %copy-done.2, bf16[64,512]{1,0:T(8,128)(2,1)S(1)} %bitcast.18, bf16[512,512]{1,0:T(8,128)(2,1)S(1)} %copy-done.1), custom_call_target="tpu_custom_call" | custom-call | tf_op jit(solution)/shard_map/sum_terms/pallas_call | solution.py:611
  184.4 0.7 copy.13
  185.0 0.6 copy.14
Async XLA Ops:
  78.5 54.5 %copy-start.1 = (bf16[512,512]{1,0:T(8,128)(2,1)S(1)}, bf16[512,512]{1,0:T(8,128)(2,1)}, u32[]{:S(2)}) copy-start(bf16[512,512]{1,0:T(8,128)(2,1)} %self_weight.1) | copy-start | bytes 1572868
  78.5 54.5 %copy-start.3 = (bf16[1,64,512]{2,1,0:T(8,128)(2,1)S(1)}, bf16[1,64,512]{2,1,0:T(8,128)(2,1)}, u32[]{:S(2)}) copy-start(bf16[1,64,512]{2,1,0:T(8,128)(2,1)} %param.9) | copy-start | bytes 196612
  133.0 2.2 %copy-start = (bf16[128,128,128]{2,1,0:T(8,128)(2,1)S(1)}, bf16[128,128,128]{2,1,0:T(8,128)(2,1)}, u32[]{:S(2)}) copy-start(bf16[128,128,128]{2,1,0:T(8,128)(2,1)} %get-tuple-element.14) | copy-start | bytes 12582916
  135.2 1.0 copy-start.2

commit v2 on v1

--- a/solution.py
+++ b/solution.py
@@ -18,7 +18,7 @@
 EDGE = 128
 FEATURE = 512
 BLOCKS = 8
-CHUNK = 16
+CHUNK = 32
 
 
 def place():
@@ -154,8 +154,6 @@
     m_copies = [push(meta, m_all.at[own], m_send.at[0], m_recv.at[0], sibling)]
     m_own = pltpu.make_async_copy(meta, m_all.at[own], local_sem.at[2])
     m_own.start()
-    t_own = pltpu.make_async_copy(tiles, t_all.at[own], local_sem.at[3])
-    t_own.start()
     t_far = []
     for h in range(2):
         there = (rel, beside * 2 + h)
@@ -282,7 +280,6 @@
     arrival(m_all.at[3], m_recv.at[1])
     arrival(m_all.at[0], m_recv.at[2])
     m_own.wait()
-    t_own.wait()
     for copy in x_second:
         copy.wait()
 
@@ -300,7 +297,7 @@
         in_specs=[ANY] * 4,
         out_specs=(ANY,) * 4,
         scratch_shapes=[
-            dma((4,)),
+            dma((3,)),
             dma((4, 3)),
             dma((4, 3)),
             dma((4, 3)),
@@ -322,94 +319,163 @@
     )(adj, layer, tiles, meta)
 
 
-def local_kernel(meta, tiles, a_rows, x_rows, weights, d_out, g_out, aw, d_sum, h_sum):
-    step = pl.program_id(0)
-    last = pl.num_programs(0) - 1
+def local_kernel(
+    meta,
+    own_tiles,
+    tiles_in,
+    a_in,
+    x_in,
+    weights_in,
+    d_out,
+    g_out,
+    tiles,
+    a_rows,
+    x_rows,
+    weights,
+    d_turned,
+    aw,
+    d_sum,
+    h_sum,
+    h_turned,
+    in_sem,
+    tile_sem,
+    out_sem,
+):
     quarter = quarter_of(lax.axis_index("node"))
-    blocks = 4 * BLOCKS
-
-    @pl.when(step == 0)
-    def _():
-        d_sum[...] = jnp.zeros_like(d_sum)
-        h_sum[...] = jnp.zeros_like(h_sum)
-        column = pl.multiple_of(quarter * QUARTER, QUARTER)
-
-        def one(b, carry):
-            rows = a_rows[b]
-            for r in range(2):
-                aw[r, b] = lax.dot_general(
-                    weights[r, pl.ds(column, QUARTER), :],
-                    rows,
-                    (((1,), (1,)), ((), ())),
-                    preferred_element_type=jnp.float32,
-                ).astype(jnp.bfloat16)
-            return carry
-
-        lax.fori_loop(0, blocks, one, 0)
-
-    slot = lax.div(step * CHUNK, TILES)
-    first = lax.rem(step * CHUNK, TILES)
-    for k in range(CHUNK):
-        code = meta[slot, 0, first + k]
-        target = slot * BLOCKS + lax.rem(code, BLOCKS)
-        relation = lax.rem(lax.div(code, BLOCKS), 2)
-        bucket = lax.div(code, 2 * BLOCKS)
-        tile = tiles[k]
-        d_sum[bucket] += jnp.dot(
-            aw[relation, target], tile, preferred_element_type=jnp.float32
-        )
-        h_sum[relation, target] += jnp.dot(
-            tile, x_rows[bucket], preferred_element_type=jnp.float32
-        )
-
-    @pl.when(step == last)
-    def _():
-        def turn(b, carry):
-            d_out[b] = d_sum[b].T.astype(jnp.bfloat16)
-            return carry
-
-        lax.fori_loop(0, NODES * BLOCKS, turn, 0)
+    shards = 4
+    buckets = NODES * BLOCKS
+    width = 4 * EDGE
+    chunks = shards * TILES // CHUNK
+    column = pl.multiple_of(quarter * QUARTER, QUARTER)
+
+    def fetch(src, dst, sem):
+        copy = pltpu.make_async_copy(src, dst, sem)
+        copy.start()
+        return copy
+
+    get_w = fetch(weights_in.at[:, pl.ds(column, QUARTER)], weights, in_sem.at[0])
+    get_a = [
+        fetch(
+            a_in.at[pl.ds(s * BLOCKS, BLOCKS)],
+            a_rows.at[pl.ds(s * BLOCKS, BLOCKS)],
+            in_sem.at[1 + s],
+        )
+        for s in range(shards)
+    ]
+    get_x = fetch(x_in, x_rows, in_sem.at[5])
+
+    core = lax.rem(lax.axis_index("node"), 2)
+    each = TILES // CHUNK
+
+    def tile_copy(n):
+        part = pl.ds(n * CHUNK, CHUNK)
+        return pltpu.make_async_copy(tiles_in.at[part], tiles.at[part], tile_sem.at[n])
+
+    for i in range(each):
+        n = (1 + core) * each + i
+        pltpu.make_async_copy(
+            own_tiles.at[pl.ds(i * CHUNK, CHUNK)],
+            tiles.at[pl.ds(n * CHUNK, CHUNK)],
+            tile_sem.at[n],
+        ).start()
+        tile_copy(i).start()
+        tile_copy((2 - core) * each + i).start()
+        tile_copy(3 * each + i).start()
+
+    d_sum[...] = jnp.zeros_like(d_sum)
+    h_sum[...] = jnp.zeros_like(h_sum)
+
+    get_w.wait()
+    both = weights[...].reshape(2 * QUARTER, FEATURE)
+    for b in range(shards * BLOCKS // 4):
+        if b % 2 == 0:
+            get_a[b // 2].wait()
+        rows = a_rows[pl.ds(b * 4, 4)].reshape(width, FEATURE)
+        value = lax.dot_general(
+            both,
+            rows,
+            (((1,), (1,)), ((), ())),
+            preferred_element_type=jnp.float32,
+        ).astype(jnp.bfloat16)
         for r in range(2):
-
-            def add(b, total):
-                turned = h_sum[r, b].T.astype(jnp.bfloat16)
-                return total + jnp.dot(
-                    turned, a_rows[b], preferred_element_type=jnp.float32
-                )
-
-            g_out[r] = lax.fori_loop(
-                0, blocks, add, jnp.zeros((QUARTER, FEATURE), jnp.float32)
-            )
-
-
-def local(meta, tiles, a_rows, x_rows, weights):
+            for i in range(4):
+                aw[r, b * 4 + i] = value[
+                    r * QUARTER : (r + 1) * QUARTER, i * EDGE : (i + 1) * EDGE
+                ]
+    get_x.wait()
+
+    def some(n, carry):
+        tile_copy(n).wait()
+        slot = lax.div(n * CHUNK, TILES)
+        first = lax.rem(n * CHUNK, TILES)
+        for k in range(CHUNK):
+            code = meta[slot, 0, first + k]
+            target = slot * BLOCKS + lax.rem(code, BLOCKS)
+            relation = lax.rem(lax.div(code, BLOCKS), 2)
+            bucket = lax.div(code, 2 * BLOCKS)
+            tile = tiles[n * CHUNK + k]
+            d_sum[bucket] += jnp.dot(
+                aw[relation, target], tile, preferred_element_type=jnp.float32
+            )
+            h_sum[relation, target] += jnp.dot(
+                tile, x_rows[bucket], preferred_element_type=jnp.float32
+            )
+        return carry
+
+    lax.fori_loop(0, chunks, some, 0)
+
+    def out_copy(n):
+        part = pl.ds(n * 16, 16)
+        return pltpu.make_async_copy(d_turned.at[part], d_out.at[part], out_sem.at[n])
+
+    def turn(n, carry):
+        for k in range(16):
+            d_turned[n * 16 + k] = d_sum[n * 16 + k].astype(jnp.bfloat16).T
+        out_copy(n).start()
+        return carry
+
+    lax.fori_loop(0, buckets // 16, turn, 0)
+    for r in range(2):
+        for b in range(shards * BLOCKS):
+            h_turned[:, pl.ds(b * EDGE, EDGE)] = h_sum[r, b].astype(jnp.bfloat16).T
+        g_out[r] = jnp.dot(
+            h_turned[...],
+            a_rows[...].reshape(shards * BLOCKS * EDGE, FEATURE),
+            preferred_element_type=jnp.float32,
+        )
+    for n in range(buckets // 16):
+        out_copy(n).wait()
+
+
+def local(meta, own_tiles, tiles, a_rows, x_rows, weights):
     buckets = NODES * BLOCKS
-    steps = 4 * TILES // CHUNK
+    shards = 4
+    bf16 = jnp.bfloat16
     return pl.pallas_call(
         local_kernel,
-        grid=(steps,),
         out_shape=(
-            jax.ShapeDtypeStruct((buckets, EDGE, QUARTER), jnp.bfloat16),
+            jax.ShapeDtypeStruct((buckets, EDGE, QUARTER), bf16),
             jax.ShapeDtypeStruct((2, QUARTER, FEATURE), jnp.float32),
         ),
-        in_specs=[
-            SMEM,
-            pl.BlockSpec((CHUNK, EDGE, EDGE), lambda s: (s, 0, 0)),
-            VMEM,
-            VMEM,
-            VMEM,
+        in_specs=[SMEM, ANY, ANY, ANY, ANY, ANY],
+        out_specs=(ANY, VMEM),
+        scratch_shapes=[
+            pltpu.VMEM((shards * TILES, EDGE, EDGE), bf16),
+            pltpu.VMEM((shards * BLOCKS, EDGE, FEATURE), bf16),
+            pltpu.VMEM((buckets, EDGE, QUARTER), bf16),
+            pltpu.VMEM((2, QUARTER, FEATURE), bf16),
+            pltpu.VMEM((buckets, EDGE, QUARTER), bf16),
+            pltpu.VMEM((2, shards * BLOCKS, QUARTER, EDGE), bf16),
+            pltpu.VMEM((buckets, QUARTER, EDGE), jnp.float32),
+            pltpu.VMEM((2, shards * BLOCKS, EDGE, QUARTER), jnp.float32),
+            pltpu.VMEM((QUARTER, shards * BLOCKS * EDGE), bf16),
+            pltpu.SemaphoreType.DMA((6,)),
+            pltpu.SemaphoreType.DMA((shards * TILES // CHUNK,)),
+            pltpu.SemaphoreType.DMA((buckets // 16,)),
         ],
-        out_specs=(VMEM, VMEM),
-        scratch_shapes=[
-            pltpu.VMEM((2, 4 * BLOCKS, QUARTER, EDGE), jnp.bfloat16),
-            pltpu.VMEM((buckets, QUARTER, EDGE), jnp.float32),
-            pltpu.VMEM((2, 4 * BLOCKS, EDGE, QUARTER), jnp.float32),
-        ],
-        compiler_params=pltpu.CompilerParams(
-            vmem_limit_bytes=56 << 20, dimension_semantics=("arbitrary",)
-        ),
+        compiler_params=pltpu.CompilerParams(vmem_limit_bytes=56 << 20),
         name="tile_products",
-    )(meta, tiles, a_rows, x_rows, weights)
+    )(meta, own_tiles, tiles, a_rows, x_rows, weights)
 
 
 def reduce_kernel(
@@ -663,6 +729,7 @@
     tiles, a_rows, x_rows, codes = gather(adj, layer_input[0], tile_values[0], meta)
     d_part, g_part = local(
         codes,
+        tile_values[0],
         tiles.reshape(4 * TILES, EDGE, EDGE),
         a_rows.reshape(4 * BLOCKS, EDGE, FEATURE),
         x_rows.reshape(NODES * BLOCKS, EDGE, QUARTER),

time: 186 us -> 124 us (0.67)
  Pallas kernels: 179 us -> 117 us
    pallas_call x1, Pallas kernels: 54.5 us -> 16.2 us  [local(): pl.pallas_call(local_kernel, out_shape=(jax.ShapeDtypeStruct((buckets, ED...]
    pallas_call x1, Pallas kernels: 76.6 us -> 53.7 us  [gather(): pl.pallas_call(gather_kernel, out_shape=(jax.ShapeDtypeStruct((4, TILES,...]
where the time goes in v2:
time: 124 us; the launch traced here: 123 us
  Pallas kernels  117 us (94%)
  local copies, waits for them, and re-layouts  5.12 us (4%)
    pallas_call x1, Pallas kernels, gather(): pl.pallas_call(gather_kernel, out_shape=(jax.ShapeDtypeStruct((4, TILES,...  53.7 us
    pallas_call x1, Pallas kernels, reduce(): pl.pallas_call(reduce_kernel, out_shape=(jax.ShapeDtypeStruct((2, 32, FEA...  46.9 us
    pallas_call x1, Pallas kernels, local(): pl.pallas_call(local_kernel, out_shape=(jax.ShapeDtypeStruct((buckets, ED...  16.2 us
    unnamed x10, local copies, waits for them, and re-layouts  4.52 us

profile of v2, /device:TPU:1, one launch (start us, length us, event | category | flops | bytes accessed | tf_op | source)
XLA Modules:
  0.0 123.4 jit_solution(9168372780601176739)
XLA Ops:
  0.6 0.7 multiply_add_fusion
  1.3 0.6 pad.4.meta
  1.9 53.7 %gather_rows_and_tiles.1 = (bf16[4,64,128,128]{3,2,1,0:T(8,128)(2,1)}, bf16[4,4,4,64,512]{4,3,2,1,0:T(8,128)(2,1)}, bf16[16,4,4,64,128]{4,3,2,1,0:T(8,128)(2,1)}, s32[4,8,128]{2,1,0:T(8,128)}) custom-call(bf16[64,512]{1,0:T(8,128)(2,1)} %bitcast.17, bf16[1024,512]{1,0:T(8,128)(2,1)} %bitcast.25, bf16[64,128,128]{2,1,0:T(8,128)(2,1)} %bitcast.21, ...), custom_call_target="tpu_custom_call" | custom-call | bytes 33554432 | tf_op jit(solution)/shard_map/gather_rows_and_tiles/pallas_call | solution.py:289
  55.7 0.0 copy-start.1
  55.7 0.0 copy-start.3
  55.7 16.2 %tile_products.1 = (bf16[128,128,128]{2,1,0:T(8,128)(2,1)}, f32[2,128,512]{2,1,0:T(8,128)}) custom-call(s32[4,8,128]{2,1,0:T(8,128)} %get-tuple-element.10.meta, bf16[64,128,128]{2,1,0:T(8,128)(2,1)} %bitcast.22, bf16[256,128,128]{2,1,0:T(8,128)(2,1)} %bitcast.20, bf16[32,128,512]{2,1,0:T(8,128)(2,1)} %bitcast.23, bf16[128,128,128]{2,1,0:T(8,128)(2,1)} %bitcast.24, ...), custom_call_target="tpu_custom_call" | custom-call | tf_op jit(solution)/shard_map/tile_products/pallas_call | solution.py:454
  71.9 0.0 copy-done.1
  72.0 0.0 copy-done.3
  72.0 0.0 copy-start
  72.0 2.2 %copy-done = bf16[128,128,128]{2,1,0:T(8,128)(2,1)S(1)} copy-done((bf16[128,128,128]{2,1,0:T(8,128)(2,1)S(1)}, bf16[128,128,128]{2,1,0:T(8,128)(2,1)}, u32[]{:S(2)}) %copy-start) | copy-done | bytes 4194328
  74.2 0.0 copy-start.2
  74.2 1.0 copy-done.2
  75.2 46.9 %sum_terms.1 = (f32[2,32,512]{2,1,0:T(8,128)S(1)}, bf16[64,512]{1,0:T(8,128)(2,1)S(1)}) custom-call(bf16[16,4,4,64,128]{4,3,2,1,0:T(8,128)(2,1)S(1)} %bitcast.16, f32[2,128,512]{2,1,0:T(8,128)S(1)} %copy-done.2, bf16[64,512]{1,0:T(8,128)(2,1)S(1)} %bitcast.18, bf16[512,512]{1,0:T(8,128)(2,1)S(1)} %copy-done.1), custom_call_target="tpu_custom_call" | custom-call | tf_op jit(solution)/shard_map/sum_terms/pallas_call | solution.py:677
  122.1 0.7 copy.13
  122.8 0.6 copy.14
Async XLA Ops:
  55.7 16.3 %copy-start.1 = (bf16[512,512]{1,0:T(8,128)(2,1)S(1)}, bf16[512,512]{1,0:T(8,128)(2,1)}, u32[]{:S(2)}) copy-start(bf16[512,512]{1,0:T(8,128)(2,1)} %self_weight.1) | copy-start | bytes 1572868
  55.7 16.3 %copy-start.3 = (bf16[1,64,512]{2,1,0:T(8,128)(2,1)S(1)}, bf16[1,64,512]{2,1,0:T(8,128)(2,1)}, u32[]{:S(2)}) copy-start(bf16[1,64,512]{2,1,0:T(8,128)(2,1)} %param.9) | copy-start | bytes 196612
  72.0 2.2 %copy-start = (bf16[128,128,128]{2,1,0:T(8,128)(2,1)S(1)}, bf16[128,128,128]{2,1,0:T(8,128)(2,1)}, u32[]{:S(2)}) copy-start(bf16[128,128,128]{2,1,0:T(8,128)(2,1)} %get-tuple-element.14) | copy-start | bytes 12582916
  74.2 1.0 copy-start.2

commit v3 on v2

v3 whole, which is shorter than its diff:
```python
import jax
import jax.numpy as jnp
from jax import lax
from jax.experimental import pallas as pl
from jax.experimental.pallas import tpu as pltpu
from jax.sharding import PartitionSpec as P

MESH = pl.DeviceIdType.MESH
ANY = pl.BlockSpec(memory_space=pl.ANY)
VMEM = pl.BlockSpec(memory_space=pltpu.VMEM)
SMEM = pl.BlockSpec(memory_space=pltpu.SMEM)

SIDE = 4
NODES = 16
ROWS = 64
QUARTER = 128
TILES = 64
EDGE = 128
FEATURE = 512
BLOCKS = 8
CHUNK = 32


def place():
    rel, node = lax.axis_index("rel"), lax.axis_index("node")
    return (
        lax.div(rel, SIDE),
        lax.rem(rel, SIDE),
        lax.div(node, 2),
        lax.rem(node, 2),
        rel,
        node,
    )


def quarter_of(node):
    return lax.rem(lax.div(node, 2), 2) * 2 + lax.rem(node, 2)


def greet(x, y, rel, node):
    barrier = pltpu.get_barrier_semaphore()

    def call(there):
        pl.semaphore_signal(barrier, inc=1, device_id=there, device_id_type=MESH)

    for k in range(1, SIDE):
        call((lax.rem(x + k, SIDE) * SIDE + y, node))
        call((x * SIDE + lax.rem(y + k, SIDE), node))
    for k in range(1, NODES):
        call((rel, lax.rem(node + k, NODES)))
    pl.semaphore_wait(barrier, 2 * (SIDE - 1) + NODES - 1)


def push(src, dst, send, recv, there):
    copy = pltpu.make_async_remote_copy(
        src_ref=src,
        dst_ref=dst,
        send_sem=send,
        recv_sem=recv,
        device_id=there,
        device_id_type=MESH,
    )
    copy.start()
    return copy


def arrival(ref, sem):
    pltpu.make_async_copy(ref, ref, sem).wait()


class RingGather:
    def __init__(self, block, at, peer, send, recv):
        self.block, self.at, self.peer, self.send, self.recv = (
            block,
            at,
            peer,
            send,
            recv,
        )
        self.copies = []

    def move(self, view, number, k):
        self.copies.append(
            push(
                view,
                view,
                self.send.at[number],
                self.recv.at[number],
                self.peer(k),
            )
        )

    def place(self, k):
        return lax.rem(self.at + k, SIDE)

    def begin(self):
        mine = self.block(self.at, None)
        self.move(mine, 0, 1)
        self.move(mine, 1, SIDE - 1)

    def forward(self):
        arrival(self.block(self.place(3), None), self.recv.at[0])
        self.move(self.block(self.place(3), 0), 2, 1)
        arrival(self.block(self.place(1), None), self.recv.at[1])
        self.move(self.block(self.place(1), 1), 3, SIDE - 1)

    def finish(self):
        arrival(self.block(self.place(2), 0), self.recv.at[2])
        arrival(self.block(self.place(2), 1), self.recv.at[3])

    def sent(self):
        for copy in self.copies:
            copy.wait_send()


def gather_kernel(
    adj,
    layer,
    tiles,
    meta,
    t_all,
    a_all,
    x_all,
    m_all,
    local_sem,
    f_send,
    f_recv,
    a_send,
    a_recv,
    x_send,
    x_recv,
    z_send,
    z_recv,
    t_send,
    t_recv,
    s_send,
    s_recv,
    m_send,
    m_recv,
):
    x, y, z, c, rel, node = place()
    half = ROWS // 2
    own = 1 + c
    near = 3 * c
    other = 2 - c
    sibling = (rel, z * 2 + (1 - c))
    beside = lax.rem(z + 7 + 2 * c, 8)
    away = 3 * (1 - c)
    quarter = quarter_of(node)
    halves = TILES // 2

    def x_peer(k):
        return (lax.rem(x + k, SIDE) * SIDE + y, node)

    def y_peer(k):
        return (x * SIDE + lax.rem(y + k, SIDE), node)

    def a_view(px, py, rows, h):
        slots = pl.ds(2 * c, 2) if h is None else 2 * c + h
        return a_all.at[slots, px, py, rows]

    every = slice(None)
    low, high = pl.ds(0, half), pl.ds(half, half)
    a_rings = (
        RingGather(
            lambda p, h: a_view(every, p, low, h), y, y_peer, a_send.at[0], a_recv.at[0]
        ),
        RingGather(
            lambda p, h: a_view(p, every, high, h), x, x_peer, a_send.at[1], a_recv.at[1]
        ),
    )

    def x_view(stream, px, py, h):
        shards = pl.ds(4 * stream, 4) if h is None else pl.ds(4 * stream + 2 * h, 2)
        return x_all.at[shards, px, py]

    def x_ring(stream, leg):
        number = 2 * stream + leg
        along_x = (stream + leg) % 2 == 0
        if along_x:
            others = y if leg == 0 else every
            return RingGather(
                lambda p, h: x_view(stream, p, others, h),
                x,
                x_peer,
                x_send.at[number],
                x_recv.at[number],
            )
        others = x if leg == 0 else every
        return RingGather(
            lambda p, h: x_view(stream, others, p, h),
            y,
            y_peer,
            x_send.at[number],
            x_recv.at[number],
        )

    x_rings = [[x_ring(stream, leg) for leg in range(2)] for stream in range(4)]

    greet(x, y, rel, node)

    a_near = push(
        adj,
        a_all.at[away, x, y],
        t_send.at[2],
        t_recv.at[2],
        (rel, beside * 2 + 1 - c),
    )

    a_first = []

    def a_send_first(source, slot, number):
        for k in range(1, SIDE):
            for rows, peer, stream in ((low, x_peer, 0), (high, y_peer, 1)):
                at = (number, stream, k - 1)
                a_first.append(
                    push(
                        source.at[rows],
                        a_all.at[slot, x, y, rows],
                        f_send.at[at],
                        f_recv.at[at],
                        peer(k),
                    )
                )

    a_send_first(adj, own, 0)
    a_own = pltpu.make_async_copy(adj, a_all.at[own, x, y], local_sem.at[0])
    a_own.start()

    z_copies = []
    for k in range(1, NODES):
        there = lax.rem(node + k, NODES)
        column = pl.multiple_of(quarter_of(there) * QUARTER, QUARTER)
        z_copies.append(
            push(
                layer.at[pl.ds(rel * ROWS, ROWS), pl.ds(column, QUARTER)],
                x_all.at[node, x, y],
                z_send.at[k - 1],
                z_recv.at[k - 1],
                (rel, there),
            )
        )
    x_own = pltpu.make_async_copy(
        layer.at[
            pl.ds(rel * ROWS, ROWS),
            pl.ds(pl.multiple_of(quarter * QUARTER, QUARTER), QUARTER),
        ],
        x_all.at[node, x, y],
        local_sem.at[1],
    )
    x_own.start()

    arrival(a_all.at[near, x, y], t_recv.at[2])
    a_send_first(a_all.at[near, x, y], near, 1)

    t_near = push(tiles, t_all.at[own], s_send.at[0], s_recv.at[0], sibling)
    m_copies = [push(meta, m_all.at[own], m_send.at[0], m_recv.at[0], sibling)]
    for h in range(2):
        m_copies.append(
            push(
                meta,
                m_all.at[away],
                m_send.at[1 + h],
                m_recv.at[1 + c],
                (rel, beside * 2 + h),
            )
        )
    m_own = pltpu.make_async_copy(meta, m_all.at[own], local_sem.at[2])
    m_own.start()

    a_own.wait()
    for copy in a_first:
        copy.wait_recv()
    for ring in a_rings:
        ring.begin()

    x_own.wait()
    for copy in z_copies:
        copy.wait_recv()
    for stream in range(4):
        x_rings[stream][0].begin()
    t_far = []
    for h in range(2):
        part = pl.ds(h * halves, halves)
        t_far.append(
            push(
                tiles.at[part],
                t_all.at[away, part],
                t_send.at[h],
                t_recv.at[c],
                (rel, beside * 2 + h),
            )
        )
    for ring in a_rings:
        ring.forward()
    for stream in range(4):
        x_rings[stream][0].forward()
    for stream in range(4):
        x_rings[stream][0].finish()
        x_rings[stream][1].begin()
    for ring in a_rings:
        ring.finish()
    pair = pl.ds(2 * c, 2)
    a_over = push(a_all.at[pair], a_all.at[pair], s_send.at[1], s_recv.at[1], sibling)
    for stream in range(4):
        x_rings[stream][1].forward()

    onward = []
    mine = pl.ds(c * halves, halves)
    for sender, slot in ((0, 3), (1, 0)):
        arrival(t_all.at[slot, mine], t_recv.at[sender])
        onward.append(
            push(
                t_all.at[slot, mine],
                t_all.at[slot, mine],
                s_send.at[2 + sender],
                s_recv.at[2 + sender],
                sibling,
            )
        )
    for stream in range(4):
        x_rings[stream][1].finish()

    arrival(t_all.at[other], s_recv.at[0])
    arrival(a_all.at[pl.ds(2 - 2 * c, 2)], s_recv.at[1])
    theirs = pl.ds((1 - c) * halves, halves)
    for sender, slot in ((0, 3), (1, 0)):
        arrival(t_all.at[slot, theirs], s_recv.at[2 + sender])
    arrival(m_all.at[other], m_recv.at[0])
    arrival(m_all.at[3], m_recv.at[1])
    arrival(m_all.at[0], m_recv.at[2])
    m_own.wait()
    for ring in a_rings:
        ring.sent()
    for rings in x_rings:
        for ring in rings:
            ring.sent()
    for copy in [a_near, t_near, a_over] + a_first + z_copies + m_copies + t_far + onward:
        copy.wait_send()


def gather(adj, layer, tiles, meta):
    dma = pltpu.SemaphoreType.DMA
    return pl.pallas_call(
        gather_kernel,
        out_shape=(
            jax.ShapeDtypeStruct((4, TILES, EDGE, EDGE), jnp.bfloat16),
            jax.ShapeDtypeStruct((4, SIDE, SIDE, ROWS, FEATURE), jnp.bfloat16),
            jax.ShapeDtypeStruct((NODES, SIDE, SIDE, ROWS, QUARTER), jnp.bfloat16),
            jax.ShapeDtypeStruct((4, 8, 128), jnp.int32),
        ),
        in_specs=[ANY] * 4,
        out_specs=(ANY,) * 4,
        scratch_shapes=[
            dma((3,)),
            dma((2, 2, 3)),
            dma((2, 2, 3)),
            dma((2, 4)),
            dma((2, 4)),
            dma((8, 4)),
            dma((8, 4)),
            dma((15,)),
            dma((15,)),
            dma((3,)),
            dma((3,)),
            dma((4,)),
            dma((4,)),
            dma((3,)),
            dma((3,)),
        ],
        compiler_params=pltpu.CompilerParams(collective_id=0, has_side_effects=True),
        cost_estimate=pl.CostEstimate(
            flops=0, bytes_accessed=32 << 20, transcendentals=0
        ),
        name="gather_rows_and_tiles",
    )(adj, layer, tiles, meta)


def local_kernel(
    meta,
    own_tiles,
    tiles_in,
    a_in,
    x_in,
    weights_in,
    d_out,
    g_out,
    tiles,
    a_rows,
    x_rows,
    weights,
    d_turned,
    aw,
    d_sum,
    h_sum,
    h_turned,
    in_sem,
    tile_sem,
    out_sem,
):
    quarter = quarter_of(lax.axis_index("node"))
    shards = 4
    buckets = NODES * BLOCKS
    width = 4 * EDGE
    chunks = shards * TILES // CHUNK
    column = pl.multiple_of(quarter * QUARTER, QUARTER)

    def fetch(src, dst, sem):
        copy = pltpu.make_async_copy(src, dst, sem)
        copy.start()
        return copy

    get_w = fetch(weights_in.at[:, pl.ds(column, QUARTER)], weights, in_sem.at[0])
    get_a = [
        fetch(
            a_in.at[pl.ds(s * BLOCKS, BLOCKS)],
            a_rows.at[pl.ds(s * BLOCKS, BLOCKS)],
            in_sem.at[1 + s],
        )
        for s in range(shards)
    ]
    get_x = fetch(x_in, x_rows, in_sem.at[5])

    core = lax.rem(lax.axis_index("node"), 2)
    each = TILES // CHUNK

    def tile_copy(n):
        part = pl.ds(n * CHUNK, CHUNK)
        return pltpu.make_async_copy(tiles_in.at[part], tiles.at[part], tile_sem.at[n])

    for i in range(each):
        n = (1 + core) * each + i
        pltpu.make_async_copy(
            own_tiles.at[pl.ds(i * CHUNK, CHUNK)],
            tiles.at[pl.ds(n * CHUNK, CHUNK)],
            tile_sem.at[n],
        ).start()
        tile_copy(i).start()
        tile_copy((2 - core) * each + i).start()
        tile_copy(3 * each + i).start()

    d_sum[...] = jnp.zeros_like(d_sum)
    h_sum[...] = jnp.zeros_like(h_sum)

    get_w.wait()
    both = weights[...].reshape(2 * QUARTER, FEATURE)
    for b in range(shards * BLOCKS // 4):
        if b % 2 == 0:
            get_a[b // 2].wait()
        rows = a_rows[pl.ds(b * 4, 4)].reshape(width, FEATURE)
        value = lax.dot_general(
            both,
            rows,
            (((1,), (1,)), ((), ())),
            preferred_element_type=jnp.float32,
        ).astype(jnp.bfloat16)
        for r in range(2):
            for i in range(4):
                aw[r, b * 4 + i] = value[
                    r * QUARTER : (r + 1) * QUARTER, i * EDGE : (i + 1) * EDGE
                ]
    get_x.wait()

    def some(n, carry):
        tile_copy(n).wait()
        slot = lax.div(n * CHUNK, TILES)
        first = lax.rem(n * CHUNK, TILES)
        for k in range(CHUNK):
            code = meta[slot, 0, first + k]
            target = slot * BLOCKS + lax.rem(code, BLOCKS)
            relation = lax.rem(lax.div(code, BLOCKS), 2)
            bucket = lax.div(code, 2 * BLOCKS)
            tile = tiles[n * CHUNK + k]
            d_sum[bucket] += jnp.dot(
                aw[relation, target], tile, preferred_element_type=jnp.float32
            )
            h_sum[relation, target] += jnp.dot(
                tile, x_rows[bucket], preferred_element_type=jnp.float32
            )
        return carry

    lax.fori_loop(0, chunks, some, 0)

    def out_copy(n):
        part = pl.ds(n * 16, 16)
        return pltpu.make_async_copy(d_turned.at[part], d_out.at[part], out_sem.at[n])

    def turn(n, carry):
        for k in range(16):
            d_turned[n * 16 + k] = d_sum[n * 16 + k].astype(jnp.bfloat16).T
        out_copy(n).start()
        return carry

    lax.fori_loop(0, buckets // 16, turn, 0)
    for r in range(2):
        for b in range(shards * BLOCKS):
            h_turned[:, pl.ds(b * EDGE, EDGE)] = h_sum[r, b].astype(jnp.bfloat16).T
        g_out[r] = jnp.dot(
            h_turned[...],
            a_rows[...].reshape(shards * BLOCKS * EDGE, FEATURE),
            preferred_element_type=jnp.float32,
        )
    for n in range(buckets // 16):
        out_copy(n).wait()


def local(meta, own_tiles, tiles, a_rows, x_rows, weights):
    buckets = NODES * BLOCKS
    shards = 4
    bf16 = jnp.bfloat16
    return pl.pallas_call(
        local_kernel,
        out_shape=(
            jax.ShapeDtypeStruct((buckets, EDGE, QUARTER), bf16),
            jax.ShapeDtypeStruct((2, QUARTER, FEATURE), jnp.float32),
        ),
        in_specs=[SMEM, ANY, ANY, ANY, ANY, ANY],
        out_specs=(ANY, VMEM),
        scratch_shapes=[
            pltpu.VMEM((shards * TILES, EDGE, EDGE), bf16),
            pltpu.VMEM((shards * BLOCKS, EDGE, FEATURE), bf16),
            pltpu.VMEM((buckets, EDGE, QUARTER), bf16),
            pltpu.VMEM((2, QUARTER, FEATURE), bf16),
            pltpu.VMEM((buckets, EDGE, QUARTER), bf16),
            pltpu.VMEM((2, shards * BLOCKS, QUARTER, EDGE), bf16),
            pltpu.VMEM((buckets, QUARTER, EDGE), jnp.float32),
            pltpu.VMEM((2, shards * BLOCKS, EDGE, QUARTER), jnp.float32),
            pltpu.VMEM((QUARTER, shards * BLOCKS * EDGE), bf16),
            pltpu.SemaphoreType.DMA((6,)),
            pltpu.SemaphoreType.DMA((shards * TILES // CHUNK,)),
            pltpu.SemaphoreType.DMA((buckets // 16,)),
        ],
        compiler_params=pltpu.CompilerParams(vmem_limit_bytes=40 << 20),
        name="tile_products",
    )(meta, own_tiles, tiles, a_rows, x_rows, weights)


class RingSum:
    def __init__(self, term, send_term, at, peer, got, out, send, recv):
        self.term, self.send_term, self.at, self.peer = term, send_term, at, peer
        self.got, self.out, self.send, self.recv = got, out, send, recv
        self.copies = []

    def place(self, k):
        return lax.rem(self.at + k, SIDE)

    def move(self, view, number, k):
        self.copies.append(
            push(
                view,
                self.got.at[number],
                self.send.at[number],
                self.recv.at[number],
                self.peer(k),
            )
        )

    def begin(self):
        self.move(self.send_term(self.place(2), 0), 0, SIDE - 1)
        self.move(self.send_term(self.place(2), 1), 1, 1)

    def direct(self):
        self.move(self.send_term(self.place(1), 0), 2, 1)
        self.move(self.send_term(self.place(3), 1), 3, SIDE - 1)

    def pass_on(self):
        for number, k, h in ((0, SIDE - 1, 0), (1, 1, 1)):
            arrival(self.got.at[number], self.recv.at[number])
            value = f32(self.term(self.place(k), h)[...]) + f32(self.got[number])
            self.out[h] = value.astype(jnp.bfloat16)
            self.move(self.out.at[h], 4 + h, k)

    def result(self, h):
        for number in (2 + h, 4 + h):
            arrival(self.got.at[number], self.recv.at[number])
        value = f32(self.got[2 + h]) + f32(self.got[4 + h])
        return (value + f32(self.term(self.at, h)[...])).astype(jnp.bfloat16)

    def sent(self):
        for copy in self.copies:
            copy.wait_send()


def f32(value):
    return value.astype(jnp.float32)


def reduce_kernel(
    d_part,
    g_part,
    adj_in,
    self_weight_in,
    g_out,
    d_out,
    d_here,
    got_first,
    out_first,
    got_second,
    out_second,
    summed,
    total,
    got_z,
    got_g,
    adj,
    self_weight,
    local_sem,
    d_sem,
    r_send,
    r_recv,
    z_send,
    z_recv,
    g_send,
    g_recv,
):
    x, y, z, c, rel, node = place()
    quarter = quarter_of(node)
    streams = 4

    def x_peer(k):
        return (lax.rem(x + k, SIDE) * SIDE + y, node)

    def y_peer(k):
        return (x * SIDE + lax.rem(y + k, SIDE), node)

    def fetch(src, dst, sem):
        copy = pltpu.make_async_copy(src, dst, sem)
        copy.start()
        return copy

    get_d = []
    for stream in range(streams):
        part = pl.ds(4 * stream, 4)
        get_d.append(fetch(d_part.at[part], d_here.at[part], d_sem.at[stream]))
    get_adj = fetch(adj_in, adj, local_sem.at[0])
    get_weight = fetch(self_weight_in, self_weight, local_sem.at[1])

    def first_ring(stream):
        along_x = stream % 2 == 0

        def view(ref, p, h):
            shards = pl.ds(4 * stream + 2 * h, 2)
            return ref.at[shards, p] if along_x else ref.at[shards, :, p]

        return RingSum(
            lambda p, h: view(d_here, p, h),
            lambda p, h: view(d_part, p, h),
            x if along_x else y,
            x_peer if along_x else y_peer,
            got_first.at[stream],
            out_first.at[stream],
            r_send.at[2 * stream],
            r_recv.at[2 * stream],
        )

    def second_ring(stream):
        along_x = stream % 2 == 1

        def view(p, h):
            return summed.at[stream, pl.ds(2 * h, 2), p]

        return RingSum(
            view,
            view,
            x if along_x else y,
            x_peer if along_x else y_peer,
            got_second.at[stream],
            out_second.at[stream],
            r_send.at[2 * stream + 1],
            r_recv.at[2 * stream + 1],
        )

    firsts = [first_ring(stream) for stream in range(streams)]
    seconds = [second_ring(stream) for stream in range(streams)]

    greet(x, y, rel, node)

    for ring in firsts:
        ring.begin()
    for ring in firsts[:2]:
        ring.direct()

    sender = lax.div(z, 2)
    for m in range(4):
        owner = quarter * 4 + m
        rows = g_part.at[:, pl.ds(32 * m, 32), :]

        @pl.when(owner != node)
        def _():
            push(
                rows,
                got_g.at[sender],
                g_send.at[m],
                g_recv.at[sender],
                (rel, owner),
            )

        @pl.when(owner == node)
        def _():
            pltpu.make_async_copy(rows, got_g.at[sender], g_recv.at[sender]).start()

    def middle(stream):
        for h in range(2):
            summed[stream, pl.ds(2 * h, 2)] = firsts[stream].result(h)
        seconds[stream].begin()
        seconds[stream].direct()

    def last(stream):
        for h in range(2):
            total[pl.ds(4 * stream + 2 * h, 2)] = seconds[stream].result(h)
        for n in range(4 * stream, 4 * stream + 4):

            @pl.when(node != n)
            def _():
                push(
                    total.at[n],
                    got_z.at[node],
                    z_send.at[n],
                    z_recv.at[node],
                    (rel, n),
                )

            @pl.when(node == n)
            def _():
                pltpu.make_async_copy(
                    total.at[n], got_z.at[node], z_recv.at[node]
                ).start()

    for stream in range(streams):
        get_d[stream].wait()
    for ring in firsts[:2]:
        ring.pass_on()
    for ring in firsts[2:]:
        ring.direct()
    for ring in firsts[2:]:
        ring.pass_on()
    middle(0)
    middle(1)
    seconds[0].pass_on()
    seconds[1].pass_on()
    middle(2)
    middle(3)
    last(0)
    last(1)
    seconds[2].pass_on()
    seconds[3].pass_on()
    last(2)
    last(3)

    get_adj.wait()
    get_weight.wait()
    own_term = lax.dot_general(
        adj[...],
        self_weight[...],
        (((1,), (1,)), ((), ())),
        preferred_element_type=jnp.float32,
    )

    for m in range(4):
        arrival(got_g.at[m], g_recv.at[m])
    g_out[...] = (got_g[0] + got_g[1]) + (got_g[2] + got_g[3])

    for n in range(NODES):
        arrival(got_z.at[n], z_recv.at[n])
    for q in range(4):
        value = own_term[:, q * QUARTER : (q + 1) * QUARTER]
        for step in range(4):
            value = value + f32(got_z[(2 * step + q // 2) * 2 + q % 2])
        d_out[:, q * QUARTER : (q + 1) * QUARTER] = value.astype(jnp.bfloat16)

    for ring in firsts + seconds:
        ring.sent()
    for m in range(4):
        owner = quarter * 4 + m

        @pl.when(owner != node)
        def _():
            pltpu.make_async_remote_copy(
                src_ref=g_part.at[:, pl.ds(32 * m, 32), :],
                dst_ref=got_g.at[sender],
                send_sem=g_send.at[m],
                recv_sem=g_recv.at[sender],
                device_id=(rel, owner),
                device_id_type=MESH,
            ).wait_send()

    for n in range(NODES):

        @pl.when(node != n)
        def _():
            pltpu.make_async_remote_copy(
                src_ref=total.at[n],
                dst_ref=got_z.at[node],
                send_sem=z_send.at[n],
                recv_sem=z_recv.at[node],
                device_id=(rel, n),
                device_id_type=MESH,
            ).wait_send()


def reduce(d_part, g_part, adj, self_weight):
    dma = pltpu.SemaphoreType.DMA
    bf16 = jnp.bfloat16
    return pl.pallas_call(
        reduce_kernel,
        out_shape=(
            jax.ShapeDtypeStruct((2, 32, FEATURE), jnp.float32),
            jax.ShapeDtypeStruct((ROWS, FEATURE), bf16),
        ),
        in_specs=[ANY, ANY, ANY, ANY],
        out_specs=(VMEM, VMEM),
        scratch_shapes=[
            pltpu.VMEM((NODES, SIDE, SIDE, ROWS, QUARTER), bf16),
            pltpu.VMEM((4, 6, 2, SIDE, ROWS, QUARTER), bf16),
            pltpu.VMEM((4, 2, 2, SIDE, ROWS, QUARTER), bf16),
            pltpu.VMEM((4, 6, 2, ROWS, QUARTER), bf16),
            pltpu.VMEM((4, 2, 2, ROWS, QUARTER), bf16),
            pltpu.VMEM((4, 4, SIDE, ROWS, QUARTER), bf16),
            pltpu.VMEM((NODES, ROWS, QUARTER), bf16),
            pltpu.VMEM((NODES, ROWS, QUARTER), bf16),
            pltpu.VMEM((4, 2, 32, FEATURE), jnp.float32),
            pltpu.VMEM((ROWS, FEATURE), bf16),
            pltpu.VMEM((FEATURE, FEATURE), bf16),
            dma((2,)),
            dma((4,)),
            dma((8, 6)),
            dma((8, 6)),
            dma((16,)),
            dma((16,)),
            dma((4,)),
            dma((4,)),
        ],
        compiler_params=pltpu.CompilerParams(
            collective_id=1, has_side_effects=True, vmem_limit_bytes=24 << 20
        ),
        name="sum_terms",
    )(d_part, g_part, adj, self_weight)


def on_device(
    out_adjoint,
    layer_input,
    rel_weights,
    self_weight,
    tile_values,
    tile_rel,
    tile_target,
    tile_src,
    tile_dest,
):
    code = (
        (tile_dest[:, :, 0] * BLOCKS + tile_src) * 2 + tile_rel
    ) * BLOCKS + tile_target
    meta = jnp.pad(code, ((0, 7), (0, 128 - TILES)))
    adj = out_adjoint[0]
    tiles, a_rows, x_rows, codes = gather(adj, layer_input[0], tile_values[0], meta)
    d_part, g_part = local(
        codes,
        tile_values[0],
        tiles.reshape(4 * TILES, EDGE, EDGE),
        a_rows.reshape(4 * BLOCKS, EDGE, FEATURE),
        x_rows.reshape(NODES * BLOCKS, EDGE, QUARTER),
        rel_weights,
    )
    rel_weight_grad, d_source = reduce(
        d_part.reshape(NODES, SIDE, SIDE, ROWS, QUARTER), g_part, adj, self_weight
    )
    return rel_weight_grad, d_source[None]


def solution(mesh):
    return jax.shard_map(
        on_device,
        mesh=mesh,
        in_specs=(
            P("node", "rel", None),
            P("node", None, None),
            P("rel", None, None),
            P(),
            P("rel", "node", None, None),
            P("rel", "node"),
            P("rel", "node"),
            P("rel", "node"),
            P("rel", "node", None),
        ),
        out_specs=(P("rel", "node", None), P("node", "rel", None)),
        check_vma=False,
    )
```

time: 124 us -> 112 us (0.903)
  Pallas kernels: 117 us -> 104 us
    pallas_call x1, Pallas kernels: 46.9 us -> 37.6 us  [reduce(): pl.pallas_call(reduce_kernel, out_shape=(jax.ShapeDtypeStruct((2, 32, FEA...]
    pallas_call x1, Pallas kernels: 16.2 us -> 13 us  [local(): pl.pallas_call(local_kernel, out_shape=(jax.ShapeDtypeStruct((buckets, ED...]
    unnamed x10 -> x14, local copies, waits for them, and re-layouts: 4.52 us -> 5.42 us
where the time goes in v3:
time: 112 us
  Pallas kernels  104 us (93%)
  local copies, waits for them, and re-layouts  6.02 us (5%)
    pallas_call x1, Pallas kernels, gather(): pl.pallas_call(gather_kernel, out_shape=(jax.ShapeDtypeStruct((4, TILES,...  53.6 us
    pallas_call x1, Pallas kernels, reduce(): pl.pallas_call(reduce_kernel, out_shape=(jax.ShapeDtypeStruct((2, 32, FEA...  37.6 us
    pallas_call x1, Pallas kernels, local(): pl.pallas_call(local_kernel, out_shape=(jax.ShapeDtypeStruct((buckets, ED...  13 us
    unnamed x14, local copies, waits for them, and re-layouts  5.42 us

profile of v3, /device:TPU:1, one launch (start us, length us, event | category | flops | bytes accessed | tf_op | source)
XLA Modules:
  0.0 111.8 jit_solution(10238276485543445220)
XLA Ops:
  0.6 0.0 copy-start
  0.6 0.9 multiply_add_fusion
  1.5 0.6 pad.4.meta
  2.1 53.6 %gather_rows_and_tiles.1 = (bf16[4,64,128,128]{3,2,1,0:T(8,128)(2,1)}, bf16[4,4,4,64,512]{4,3,2,1,0:T(8,128)(2,1)}, bf16[16,4,4,64,128]{4,3,2,1,0:T(8,128)(2,1)}, s32[4,8,128]{2,1,0:T(8,128)}) custom-call(bf16[64,512]{1,0:T(8,128)(2,1)} %bitcast.20, bf16[1024,512]{1,0:T(8,128)(2,1)} %bitcast.25, bf16[64,128,128]{2,1,0:T(8,128)(2,1)} %bitcast.16, ...), custom_call_target="tpu_custom_call" | custom-call | bytes 33554432 | tf_op jit(solution)/shard_map/gather_rows_and_tiles/pallas_call | solution.py:344
  55.7 0.0 copy-done
  55.7 0.0 copy-start.1
  55.7 2.2 %copy-done.1 = bf16[4,4,4,64,512]{4,3,2,1,0:T(8,128)(2,1)S(1)} copy-done((bf16[4,4,4,64,512]{4,3,2,1,0:T(8,128)(2,1)S(1)}, bf16[4,4,4,64,512]{4,3,2,1,0:T(8,128)(2,1)}, u32[]{:S(2)}) %copy-start.1) | copy-done | bytes 4194328
  57.9 0.0 copy-start.2
  57.9 1.2 %copy-done.2 = bf16[2,512,512]{2,1,0:T(8,128)(2,1)S(1)} copy-done((bf16[2,512,512]{2,1,0:T(8,128)(2,1)S(1)}, bf16[2,512,512]{2,1,0:T(8,128)(2,1)}, u32[]{:S(2)}) %copy-start.2) | copy-done | bytes 1048600
  59.1 0.0 copy-start.5
  59.1 0.7 copy-done.5
  59.8 0.0 copy-start.3
  59.8 0.0 copy-start.4
  59.8 13.0 %tile_products.1 = (bf16[128,128,128]{2,1,0:T(8,128)(2,1)S(1)}, f32[2,128,512]{2,1,0:T(8,128)S(1)}) custom-call(s32[4,8,128]{2,1,0:T(8,128)S(1)} %copy-done.5, bf16[64,128,128]{2,1,0:T(8,128)(2,1)S(1)} %bitcast.17, bf16[256,128,128]{2,1,0:T(8,128)(2,1)} %bitcast.23, bf16[32,128,512]{2,1,0:T(8,128)(2,1)S(1)} %bitcast.19, bf16[128,128,128]{2,1,0:T(8,128)(2,1)} %bitcast.24, ...), custom_call_target="tpu_custom_call" | custom-call | tf_op jit(solution)/shard_map/tile_products/pallas_call | solution.py:511
  72.9 0.0 copy-done.3
  72.9 0.0 copy-done.4
  72.9 37.6 %sum_terms.1 = (f32[2,32,512]{2,1,0:T(8,128)S(1)}, bf16[64,512]{1,0:T(8,128)(2,1)S(1)}) custom-call(bf16[16,4,4,64,128]{4,3,2,1,0:T(8,128)(2,1)S(1)} %bitcast.18, f32[2,128,512]{2,1,0:T(8,128)S(1)} %get-tuple-element.15.g_part, bf16[64,512]{1,0:T(8,128)(2,1)S(1)} %bitcast.21, bf16[512,512]{1,0:T(8,128)(2,1)S(1)} %copy-done.3), custom_call_target="tpu_custom_call" | custom-call | tf_op jit(solution)/shard_map/sum_terms/pallas_call | solution.py:803
  110.5 0.7 copy.13
  111.1 0.6 copy.14
Async XLA Ops:
  0.6 55.0 %copy-start = (bf16[1,64,128,128]{3,2,1,0:T(8,128)(2,1)S(1)}, bf16[1,64,128,128]{3,2,1,0:T(8,128)(2,1)}, u32[]{:S(2)}) copy-start(bf16[1,64,128,128]{3,2,1,0:T(8,128)(2,1)} %param.13) | copy-start | bytes 6291460
  55.7 2.2 %copy-start.1 = (bf16[4,4,4,64,512]{4,3,2,1,0:T(8,128)(2,1)S(1)}, bf16[4,4,4,64,512]{4,3,2,1,0:T(8,128)(2,1)}, u32[]{:S(2)}) copy-start(bf16[4,4,4,64,512]{4,3,2,1,0:T(8,128)(2,1)} %get-tuple-element.12) | copy-start | bytes 12582916
  57.9 1.2 %copy-start.2 = (bf16[2,512,512]{2,1,0:T(8,128)(2,1)S(1)}, bf16[2,512,512]{2,1,0:T(8,128)(2,1)}, u32[]{:S(2)}) copy-start(bf16[2,512,512]{2,1,0:T(8,128)(2,1)} %weights_in.1) | copy-start | bytes 3145732
  59.1 0.7 copy-start.5
  59.8 13.1 %copy-start.3 = (bf16[512,512]{1,0:T(8,128)(2,1)S(1)}, bf16[512,512]{1,0:T(8,128)(2,1)}, u32[]{:S(2)}) copy-start(bf16[512,512]{1,0:T(8,128)(2,1)} %self_weight_in.1) | copy-start | bytes 1572868
  59.8 13.1 %copy-start.4 = (bf16[1,64,512]{2,1,0:T(8,128)(2,1)S(1)}, bf16[1,64,512]{2,1,0:T(8,128)(2,1)}, u32[]{:S(2)}) copy-start(bf16[1,64,512]{2,1,0:T(8,128)(2,1)} %param.9) | copy-start | bytes 196612

commit v4 on v3

--- a/solution.py
+++ b/solution.py
@@ -1,3 +1,5 @@
+import functools
+
 import jax
 import jax.numpy as jnp
 from jax import lax
@@ -8,7 +10,7 @@
 MESH = pl.DeviceIdType.MESH
 ANY = pl.BlockSpec(memory_space=pl.ANY)
 VMEM = pl.BlockSpec(memory_space=pltpu.VMEM)
-SMEM = pl.BlockSpec(memory_space=pltpu.SMEM)
+HBM = pl.BlockSpec(memory_space=pltpu.HBM)
 
 SIDE = 4
 NODES = 16
@@ -146,7 +148,6 @@
     sibling = (rel, z * 2 + (1 - c))
     beside = lax.rem(z + 7 + 2 * c, 8)
     away = 3 * (1 - c)
-    quarter = quarter_of(node)
     halves = TILES // 2
 
     def x_peer(k):
@@ -155,24 +156,38 @@
     def y_peer(k):
         return (x * SIDE + lax.rem(y + k, SIDE), node)
 
-    def a_view(px, py, rows, h):
-        slots = pl.ds(2 * c, 2) if h is None else 2 * c + h
-        return a_all.at[slots, px, py, rows]
-
     every = slice(None)
     low, high = pl.ds(0, half), pl.ds(half, half)
-    a_rings = (
-        RingGather(
-            lambda p, h: a_view(every, p, low, h), y, y_peer, a_send.at[0], a_recv.at[0]
-        ),
-        RingGather(
-            lambda p, h: a_view(p, every, high, h), x, x_peer, a_send.at[1], a_recv.at[1]
-        ),
-    )
+
+    def part_of(h):
+        return every if h is None else pl.ds(2 * h, 2)
+
+    def second_leg(slot, number):
+        return (
+            RingGather(
+                lambda p, h: a_all.at[slot, part_of(h), p, low],
+                y,
+                y_peer,
+                a_send.at[number, 0],
+                a_recv.at[number, 0],
+            ),
+            RingGather(
+                lambda p, h: a_all.at[slot, p, part_of(h), high],
+                x,
+                x_peer,
+                a_send.at[number, 1],
+                a_recv.at[number, 1],
+            ),
+        )
+
+    a_rings = (second_leg(own, 0), second_leg(near, 1))
+
+    streams = ((2, 4, 2), (6, 4, 2), (10, 3, 2), (13, 3, 1))
 
     def x_view(stream, px, py, h):
-        shards = pl.ds(4 * stream, 4) if h is None else pl.ds(4 * stream + 2 * h, 2)
-        return x_all.at[shards, px, py]
+        base, count, cut = streams[stream]
+        shards = (pl.ds(base, cut), pl.ds(base + cut, count - cut))
+        return x_all.at[pl.ds(base, count) if h is None else shards[h], px, py]
 
     def x_ring(stream, leg):
         number = 2 * stream + leg
@@ -207,13 +222,13 @@
         (rel, beside * 2 + 1 - c),
     )
 
-    a_first = []
+    a_first = ([], [])
 
     def a_send_first(source, slot, number):
         for k in range(1, SIDE):
             for rows, peer, stream in ((low, x_peer, 0), (high, y_peer, 1)):
                 at = (number, stream, k - 1)
-                a_first.append(
+                a_first[number].append(
                     push(
                         source.at[rows],
                         a_all.at[slot, x, y, rows],
@@ -227,28 +242,23 @@
     a_own = pltpu.make_async_copy(adj, a_all.at[own, x, y], local_sem.at[0])
     a_own.start()
 
+    def columns(there):
+        return pl.ds(pl.multiple_of(quarter_of(there) * QUARTER, QUARTER), QUARTER)
+
     z_copies = []
-    for k in range(1, NODES):
-        there = lax.rem(node + k, NODES)
-        column = pl.multiple_of(quarter_of(there) * QUARTER, QUARTER)
-        z_copies.append(
-            push(
-                layer.at[pl.ds(rel * ROWS, ROWS), pl.ds(column, QUARTER)],
-                x_all.at[node, x, y],
-                z_send.at[k - 1],
-                z_recv.at[k - 1],
-                (rel, there),
+    for k in (1, 7, 2, 6, 3, 5, 4):
+        for core in range(2):
+            there = lax.rem(z + k, 8) * 2 + core
+            index = (8 - k) * 2 + c
+            z_copies.append(
+                push(
+                    layer.at[x, y, :, columns(there)],
+                    x_all.at[index, x, y],
+                    z_send.at[2 * k + core - 2],
+                    z_recv.at[index - 2],
+                    (rel, there),
+                )
             )
-        )
-    x_own = pltpu.make_async_copy(
-        layer.at[
-            pl.ds(rel * ROWS, ROWS),
-            pl.ds(pl.multiple_of(quarter * QUARTER, QUARTER), QUARTER),
-        ],
-        x_all.at[node, x, y],
-        local_sem.at[1],
-    )
-    x_own.start()
 
     arrival(a_all.at[near, x, y], t_recv.at[2])
     a_send_first(a_all.at[near, x, y], near, 1)
@@ -268,16 +278,29 @@
     m_own = pltpu.make_async_copy(meta, m_all.at[own], local_sem.at[2])
     m_own.start()
 
+    x_near = push(
+        layer.at[:, :, :, columns(z * 2 + 1 - c)],
+        x_all.at[c],
+        s_send.at[4],
+        s_recv.at[4],
+        sibling,
+    )
+    x_own = pltpu.make_async_copy(
+        layer.at[:, :, :, columns(node)], x_all.at[c], local_sem.at[1]
+    )
+    x_own.start()
+
     a_own.wait()
-    for copy in a_first:
-        copy.wait_recv()
-    for ring in a_rings:
-        ring.begin()
-
-    x_own.wait()
-    for copy in z_copies:
-        copy.wait_recv()
+    for number in range(2):
+        for copy in a_first[number]:
+            copy.wait_recv()
+        for ring in a_rings[number]:
+            ring.begin()
+
     for stream in range(4):
+        base, count, _ = streams[stream]
+        for index in range(base, base + count):
+            arrival(x_all.at[index, x, y], z_recv.at[index - 2])
         x_rings[stream][0].begin()
     t_far = []
     for h in range(2):
@@ -291,14 +314,14 @@
                 (rel, beside * 2 + h),
             )
         )
-    for ring in a_rings:
+    for ring in a_rings[0] + a_rings[1]:
         ring.forward()
     for stream in range(4):
         x_rings[stream][0].forward()
     for stream in range(4):
         x_rings[stream][0].finish()
         x_rings[stream][1].begin()
-    for ring in a_rings:
+    for ring in a_rings[0] + a_rings[1]:
         ring.finish()
     pair = pl.ds(2 * c, 2)
     a_over = push(a_all.at[pair], a_all.at[pair], s_send.at[1], s_recv.at[1], sibling)
@@ -330,12 +353,22 @@
     arrival(m_all.at[3], m_recv.at[1])
     arrival(m_all.at[0], m_recv.at[2])
     m_own.wait()
-    for ring in a_rings:
+    x_own.wait()
+    arrival(x_all.at[1 - c], s_recv.at[4])
+    for ring in a_rings[0] + a_rings[1]:
         ring.sent()
     for rings in x_rings:
         for ring in rings:
             ring.sent()
-    for copy in [a_near, t_near, a_over] + a_first + z_copies + m_copies + t_far + onward:
+    for copy in (
+        [a_near, t_near, a_over, x_near]
+        + a_first[0]
+        + a_first[1]
+        + z_copies
+        + m_copies
+        + t_far
+        + onward
+    ):
         copy.wait_send()
 
 
@@ -355,16 +388,16 @@
             dma((3,)),
             dma((2, 2, 3)),
             dma((2, 2, 3)),
-            dma((2, 4)),
-            dma((2, 4)),
+            dma((2, 2, 4)),
+            dma((2, 2, 4)),
             dma((8, 4)),
             dma((8, 4)),
-            dma((15,)),
-            dma((15,)),
+            dma((14,)),
+            dma((14,)),
             dma((3,)),
             dma((3,)),
-            dma((4,)),
-            dma((4,)),
+            dma((5,)),
+            dma((5,)),
             dma((3,)),
             dma((3,)),
         ],
@@ -377,7 +410,7 @@
 
 
 def local_kernel(
-    meta,
+    meta_in,
     own_tiles,
     tiles_in,
     a_in,
@@ -394,6 +427,7 @@
     d_sum,
     h_sum,
     h_turned,
+    meta,
     in_sem,
     tile_sem,
     out_sem,
@@ -410,6 +444,7 @@
         copy.start()
         return copy
 
+    get_meta = fetch(meta_in, meta, in_sem.at[6])
     get_w = fetch(weights_in.at[:, pl.ds(column, QUARTER)], weights, in_sem.at[0])
     get_a = [
         fetch(
@@ -422,6 +457,7 @@
     get_x = fetch(x_in, x_rows, in_sem.at[5])
 
     core = lax.rem(lax.axis_index("node"), 2)
+    chip = lax.div(lax.axis_index("node"), 2)
     each = TILES // CHUNK
 
     def tile_copy(n):
@@ -460,6 +496,7 @@
                     r * QUARTER : (r + 1) * QUARTER, i * EDGE : (i + 1) * EDGE
                 ]
     get_x.wait()
+    get_meta.wait()
 
     def some(n, carry):
         tile_copy(n).wait()
@@ -475,7 +512,8 @@
                 aw[relation, target], tile, preferred_element_type=jnp.float32
             )
             h_sum[relation, target] += jnp.dot(
-                tile, x_rows[bucket], preferred_element_type=jnp.float32
+                tile, x_rows[jnp.bitwise_and(bucket - 16 * chip, 127)],
+                preferred_element_type=jnp.float32
             )
         return carry
 
@@ -514,7 +552,7 @@
             jax.ShapeDtypeStruct((buckets, EDGE, QUARTER), bf16),
             jax.ShapeDtypeStruct((2, QUARTER, FEATURE), jnp.float32),
         ),
-        in_specs=[SMEM, ANY, ANY, ANY, ANY, ANY],
+        in_specs=[HBM, ANY, HBM, HBM, HBM, HBM],
         out_specs=(ANY, VMEM),
         scratch_shapes=[
             pltpu.VMEM((shards * TILES, EDGE, EDGE), bf16),
@@ -526,7 +564,8 @@
             pltpu.VMEM((buckets, QUARTER, EDGE), jnp.float32),
             pltpu.VMEM((2, shards * BLOCKS, EDGE, QUARTER), jnp.float32),
             pltpu.VMEM((QUARTER, shards * BLOCKS * EDGE), bf16),
-            pltpu.SemaphoreType.DMA((6,)),
+            pltpu.SMEM((shards, 8, 128), jnp.int32),
+            pltpu.SemaphoreType.DMA((7,)),
             pltpu.SemaphoreType.DMA((shards * TILES // CHUNK,)),
             pltpu.SemaphoreType.DMA((buckets // 16,)),
         ],
@@ -852,14 +891,22 @@
     ) * BLOCKS + tile_target
     meta = jnp.pad(code, ((0, 7), (0, 128 - TILES)))
     adj = out_adjoint[0]
-    tiles, a_rows, x_rows, codes = gather(adj, layer_input[0], tile_values[0], meta)
+    tiles, a_rows, x_rows, codes = gather(
+        adj,
+        layer_input.reshape(SIDE, SIDE, ROWS, FEATURE),
+        tile_values[0],
+        meta,
+    )
+    stay = functools.partial(
+        pltpu.with_memory_space_constraint, memory_space=pltpu.HBM
+    )
     d_part, g_part = local(
-        codes,
+        stay(codes),
         tile_values[0],
-        tiles.reshape(4 * TILES, EDGE, EDGE),
-        a_rows.reshape(4 * BLOCKS, EDGE, FEATURE),
-        x_rows.reshape(NODES * BLOCKS, EDGE, QUARTER),
-        rel_weights,
+        stay(tiles.reshape(4 * TILES, EDGE, EDGE)),
+        stay(a_rows.reshape(4 * BLOCKS, EDGE, FEATURE)),
+        stay(x_rows.reshape(NODES * BLOCKS, EDGE, QUARTER)),
+        stay(rel_weights),
     )
     rel_weight_grad, d_source = reduce(
         d_part.reshape(NODES, SIDE, SIDE, ROWS, QUARTER), g_part, adj, self_weight

time: 112 us -> 104 us (0.929)
  local copies, waits for them, and re-layouts: 6.02 us -> 1.9 us
  Pallas kernels: 104 us -> 101 us
    unnamed x14 -> x8, local copies, waits for them, and re-layouts: 5.42 us -> 1.31 us
    pallas_call x1, Pallas kernels: 53.6 us -> 49.9 us  [gather(): pl.pallas_call(gather_kernel, out_shape=(jax.ShapeDtypeStruct((4, TILES,...]
where the time goes in v4:
time: 104 us
  Pallas kernels  101 us (97%)
  local copies, waits for them, and re-layouts  1.9 us (2%)
    pallas_call x1, Pallas kernels, gather(): pl.pallas_call(gather_kernel, out_shape=(jax.ShapeDtypeStruct((4, TILES,...  49.9 us
    pallas_call x1, Pallas kernels, reduce(): pl.pallas_call(reduce_kernel, out_shape=(jax.ShapeDtypeStruct((2, 32, FEA...  37.5 us
    pallas_call x1, Pallas kernels, local(): pl.pallas_call(local_kernel, out_shape=(jax.ShapeDtypeStruct((buckets, ED...  13.1 us

profile of v4, /device:TPU:1, one launch (start us, length us, event | category | flops | bytes accessed | tf_op | source)
XLA Modules:
  0.0 104.0 jit_solution(3559947512010761715)
XLA Ops:
  0.6 0.0 copy-start
  0.6 0.9 multiply_add_fusion
  1.5 0.6 pad.4.meta
  2.1 49.9 %gather_rows_and_tiles.1 = (bf16[4,64,128,128]{3,2,1,0:T(8,128)(2,1)}, bf16[4,4,4,64,512]{4,3,2,1,0:T(8,128)(2,1)}, bf16[16,4,4,64,128]{4,3,2,1,0:T(8,128)(2,1)}, s32[4,8,128]{2,1,0:T(8,128)}) custom-call(bf16[64,512]{1,0:T(8,128)(2,1)} %bitcast.19, bf16[4,4,64,512]{3,2,1,0:T(8,128)(2,1)} %bitcast.25, bf16[64,128,128]{2,1,0:T(8,128)(2,1)} %bitcast.16, ...), custom_call_target="tpu_custom_call" | custom-call | bytes 33554432 | tf_op jit(solution)/shard_map/gather_rows_and_tiles/pallas_call | solution.py:377
  52.0 0.0 copy-done
  52.0 0.0 copy-start.1
  52.0 0.0 copy-start.2
  52.0 13.1 %tile_products.1 = (bf16[128,128,128]{2,1,0:T(8,128)(2,1)S(1)}, f32[2,128,512]{2,1,0:T(8,128)S(1)}) custom-call(s32[4,8,128]{2,1,0:T(8,128)} %get-tuple-element.10.meta_in, bf16[64,128,128]{2,1,0:T(8,128)(2,1)S(1)} %bitcast.17, bf16[256,128,128]{2,1,0:T(8,128)(2,1)} %bitcast.22, bf16[32,128,512]{2,1,0:T(8,128)(2,1)} %bitcast.23, ...), custom_call_target="tpu_custom_call" | custom-call | tf_op jit(solution)/shard_map/tile_products/pallas_call | solution.py:549
  65.2 0.0 copy-done.1
  65.2 0.0 copy-done.2
  65.2 37.5 %sum_terms.1 = (f32[2,32,512]{2,1,0:T(8,128)S(1)}, bf16[64,512]{1,0:T(8,128)(2,1)S(1)}) custom-call(bf16[16,4,4,64,128]{4,3,2,1,0:T(8,128)(2,1)S(1)} %bitcast.18, f32[2,128,512]{2,1,0:T(8,128)S(1)} %get-tuple-element.15.g_part, bf16[64,512]{1,0:T(8,128)(2,1)S(1)} %bitcast.20, bf16[512,512]{1,0:T(8,128)(2,1)S(1)} %copy-done.1), custom_call_target="tpu_custom_call" | custom-call | tf_op jit(solution)/shard_map/sum_terms/pallas_call | solution.py:842
  102.7 0.7 copy.13
  103.4 0.6 copy.14
Async XLA Ops:
  0.6 51.4 %copy-start = (bf16[1,64,128,128]{3,2,1,0:T(8,128)(2,1)S(1)}, bf16[1,64,128,128]{3,2,1,0:T(8,128)(2,1)}, u32[]{:S(2)}) copy-start(bf16[1,64,128,128]{3,2,1,0:T(8,128)(2,1)} %param.13) | copy-start | bytes 6291460
  52.0 13.2 %copy-start.1 = (bf16[512,512]{1,0:T(8,128)(2,1)S(1)}, bf16[512,512]{1,0:T(8,128)(2,1)}, u32[]{:S(2)}) copy-start(bf16[512,512]{1,0:T(8,128)(2,1)} %self_weight_in.1) | copy-start | bytes 1572868
  52.0 13.1 %copy-start.2 = (bf16[1,64,512]{2,1,0:T(8,128)(2,1)S(1)}, bf16[1,64,512]{2,1,0:T(8,128)(2,1)}, u32[]{:S(2)}) copy-start(bf16[1,64,512]{2,1,0:T(8,128)(2,1)} %param.9) | copy-start | bytes 196612

commit v5 on v4

--- a/solution.py
+++ b/solution.py
@@ -383,7 +383,7 @@
             jax.ShapeDtypeStruct((4, 8, 128), jnp.int32),
         ),
         in_specs=[ANY] * 4,
-        out_specs=(ANY,) * 4,
+        out_specs=(VMEM, VMEM, VMEM, ANY),
         scratch_shapes=[
             dma((3,)),
             dma((2, 2, 3)),
@@ -401,7 +401,9 @@
             dma((3,)),
             dma((3,)),
         ],
-        compiler_params=pltpu.CompilerParams(collective_id=0, has_side_effects=True),
+        compiler_params=pltpu.CompilerParams(
+            collective_id=0, has_side_effects=True, vmem_limit_bytes=24 << 20
+        ),
         cost_estimate=pl.CostEstimate(
             flops=0, bytes_accessed=32 << 20, transcendentals=0
         ),
@@ -412,31 +414,24 @@
 def local_kernel(
     meta_in,
     own_tiles,
-    tiles_in,
-    a_in,
-    x_in,
+    tiles,
+    a_rows,
+    x_rows,
     weights_in,
     d_out,
     g_out,
-    tiles,
-    a_rows,
-    x_rows,
     weights,
-    d_turned,
     aw,
     d_sum,
     h_sum,
     h_turned,
     meta,
     in_sem,
-    tile_sem,
-    out_sem,
 ):
     quarter = quarter_of(lax.axis_index("node"))
     shards = 4
     buckets = NODES * BLOCKS
     width = 4 * EDGE
-    chunks = shards * TILES // CHUNK
     column = pl.multiple_of(quarter * QUARTER, QUARTER)
 
     def fetch(src, dst, sem):
@@ -444,45 +439,18 @@
         copy.start()
         return copy
 
-    get_meta = fetch(meta_in, meta, in_sem.at[6])
-    get_w = fetch(weights_in.at[:, pl.ds(column, QUARTER)], weights, in_sem.at[0])
-    get_a = [
-        fetch(
-            a_in.at[pl.ds(s * BLOCKS, BLOCKS)],
-            a_rows.at[pl.ds(s * BLOCKS, BLOCKS)],
-            in_sem.at[1 + s],
-        )
-        for s in range(shards)
-    ]
-    get_x = fetch(x_in, x_rows, in_sem.at[5])
-
+    get_meta = fetch(meta_in, meta, in_sem.at[0])
+    get_w = fetch(weights_in.at[:, pl.ds(column, QUARTER)], weights, in_sem.at[1])
     core = lax.rem(lax.axis_index("node"), 2)
     chip = lax.div(lax.axis_index("node"), 2)
     each = TILES // CHUNK
 
-    def tile_copy(n):
-        part = pl.ds(n * CHUNK, CHUNK)
-        return pltpu.make_async_copy(tiles_in.at[part], tiles.at[part], tile_sem.at[n])
-
-    for i in range(each):
-        n = (1 + core) * each + i
-        pltpu.make_async_copy(
-            own_tiles.at[pl.ds(i * CHUNK, CHUNK)],
-            tiles.at[pl.ds(n * CHUNK, CHUNK)],
-            tile_sem.at[n],
-        ).start()
-        tile_copy(i).start()
-        tile_copy((2 - core) * each + i).start()
-        tile_copy(3 * each + i).start()
-
     d_sum[...] = jnp.zeros_like(d_sum)
     h_sum[...] = jnp.zeros_like(h_sum)
 
     get_w.wait()
     both = weights[...].reshape(2 * QUARTER, FEATURE)
     for b in range(shards * BLOCKS // 4):
-        if b % 2 == 0:
-            get_a[b // 2].wait()
         rows = a_rows[pl.ds(b * 4, 4)].reshape(width, FEATURE)
         value = lax.dot_general(
             both,
@@ -495,38 +463,44 @@
                 aw[r, b * 4 + i] = value[
                     r * QUARTER : (r + 1) * QUARTER, i * EDGE : (i + 1) * EDGE
                 ]
-    get_x.wait()
     get_meta.wait()
 
-    def some(n, carry):
-        tile_copy(n).wait()
+    def some(n, source, start):
         slot = lax.div(n * CHUNK, TILES)
         first = lax.rem(n * CHUNK, TILES)
         for k in range(CHUNK):
             code = meta[slot, 0, first + k]
             target = slot * BLOCKS + lax.rem(code, BLOCKS)
             relation = lax.rem(lax.div(code, BLOCKS), 2)
-            bucket = lax.div(code, 2 * BLOCKS)
-            tile = tiles[n * CHUNK + k]
+            bucket = jnp.bitwise_and(
+                lax.div(code, 2 * BLOCKS) - 16 * chip, buckets - 1
+            )
+            tile = source[start + k]
             d_sum[bucket] += jnp.dot(
                 aw[relation, target], tile, preferred_element_type=jnp.float32
             )
             h_sum[relation, target] += jnp.dot(
-                tile, x_rows[jnp.bitwise_and(bucket - 16 * chip, 127)],
-                preferred_element_type=jnp.float32
-            )
+                tile, x_rows[bucket], preferred_element_type=jnp.float32
+            )
+
+    def own_some(i, carry):
+        some((1 + core) * each + i, own_tiles, i * CHUNK)
         return carry
 
-    lax.fori_loop(0, chunks, some, 0)
-
-    def out_copy(n):
-        part = pl.ds(n * 16, 16)
-        return pltpu.make_async_copy(d_turned.at[part], d_out.at[part], out_sem.at[n])
+    def other_some(i, carry):
+        number = lax.div(i, each)
+        slot = lax.rem(4 - core * lax.rem(number, 2) + 2 * lax.rem(number, 2), 4)
+        slot = jnp.where(number == 2, 3, slot)
+        n = slot * each + lax.rem(i, each)
+        some(n, tiles, n * CHUNK)
+        return carry
+
+    lax.fori_loop(0, each, own_some, 0)
+    lax.fori_loop(0, 3 * each, other_some, 0)
 
     def turn(n, carry):
         for k in range(16):
-            d_turned[n * 16 + k] = d_sum[n * 16 + k].astype(jnp.bfloat16).T
-        out_copy(n).start()
+            d_out[n * 16 + k] = d_sum[n * 16 + k].astype(jnp.bfloat16).T
         return carry
 
     lax.fori_loop(0, buckets // 16, turn, 0)
@@ -538,8 +512,6 @@
             a_rows[...].reshape(shards * BLOCKS * EDGE, FEATURE),
             preferred_element_type=jnp.float32,
         )
-    for n in range(buckets // 16):
-        out_copy(n).wait()
 
 
 def local(meta, own_tiles, tiles, a_rows, x_rows, weights):
@@ -552,24 +524,18 @@
             jax.ShapeDtypeStruct((buckets, EDGE, QUARTER), bf16),
             jax.ShapeDtypeStruct((2, QUARTER, FEATURE), jnp.float32),
         ),
-        in_specs=[HBM, ANY, HBM, HBM, HBM, HBM],
-        out_specs=(ANY, VMEM),
+        in_specs=[HBM, VMEM, VMEM, VMEM, VMEM, HBM],
+        out_specs=(VMEM, VMEM),
         scratch_shapes=[
-            pltpu.VMEM((shards * TILES, EDGE, EDGE), bf16),
-            pltpu.VMEM((shards * BLOCKS, EDGE, FEATURE), bf16),
-            pltpu.VMEM((buckets, EDGE, QUARTER), bf16),
             pltpu.VMEM((2, QUARTER, FEATURE), bf16),
-            pltpu.VMEM((buckets, EDGE, QUARTER), bf16),
             pltpu.VMEM((2, shards * BLOCKS, QUARTER, EDGE), bf16),
             pltpu.VMEM((buckets, QUARTER, EDGE), jnp.float32),
             pltpu.VMEM((2, shards * BLOCKS, EDGE, QUARTER), jnp.float32),
             pltpu.VMEM((QUARTER, shards * BLOCKS * EDGE), bf16),
             pltpu.SMEM((shards, 8, 128), jnp.int32),
-            pltpu.SemaphoreType.DMA((7,)),
-            pltpu.SemaphoreType.DMA((shards * TILES // CHUNK,)),
-            pltpu.SemaphoreType.DMA((buckets // 16,)),
+            pltpu.SemaphoreType.DMA((2,)),
         ],
-        compiler_params=pltpu.CompilerParams(vmem_limit_bytes=40 << 20),
+        compiler_params=pltpu.CompilerParams(vmem_limit_bytes=24 << 20),
         name="tile_products",
     )(meta, own_tiles, tiles, a_rows, x_rows, weights)
 
@@ -631,11 +597,9 @@
     self_weight_in,
     g_out,
     d_out,
-    d_here,
     got_first,
     out_first,
     got_second,
-    out_second,
     summed,
     total,
     got_z,
@@ -643,9 +607,10 @@
     adj,
     self_weight,
     local_sem,
-    d_sem,
     r_send,
     r_recv,
+    q_send,
+    q_recv,
     z_send,
     z_recv,
     g_send,
@@ -666,10 +631,6 @@
         copy.start()
         return copy
 
-    get_d = []
-    for stream in range(streams):
-        part = pl.ds(4 * stream, 4)
-        get_d.append(fetch(d_part.at[part], d_here.at[part], d_sem.at[stream]))
     get_adj = fetch(adj_in, adj, local_sem.at[0])
     get_weight = fetch(self_weight_in, self_weight, local_sem.at[1])
 
@@ -681,41 +642,23 @@
             return ref.at[shards, p] if along_x else ref.at[shards, :, p]
 
         return RingSum(
-            lambda p, h: view(d_here, p, h),
+            lambda p, h: view(d_part, p, h),
             lambda p, h: view(d_part, p, h),
             x if along_x else y,
             x_peer if along_x else y_peer,
             got_first.at[stream],
             out_first.at[stream],
-            r_send.at[2 * stream],
-            r_recv.at[2 * stream],
-        )
-
-    def second_ring(stream):
-        along_x = stream % 2 == 1
-
-        def view(p, h):
-            return summed.at[stream, pl.ds(2 * h, 2), p]
-
-        return RingSum(
-            view,
-            view,
-            x if along_x else y,
-            x_peer if along_x else y_peer,
-            got_second.at[stream],
-            out_second.at[stream],
-            r_send.at[2 * stream + 1],
-            r_recv.at[2 * stream + 1],
+            r_send.at[stream],
+            r_recv.at[stream],
         )
 
     firsts = [first_ring(stream) for stream in range(streams)]
-    seconds = [second_ring(stream) for stream in range(streams)]
 
     greet(x, y, rel, node)
 
     for ring in firsts:
         ring.begin()
-    for ring in firsts[:2]:
+    for ring in firsts:
         ring.direct()
 
     sender = lax.div(z, 2)
@@ -737,51 +680,55 @@
         def _():
             pltpu.make_async_copy(rows, got_g.at[sender], g_recv.at[sender]).start()
 
+    later = []
+
     def middle(stream):
         for h in range(2):
             summed[stream, pl.ds(2 * h, 2)] = firsts[stream].result(h)
-        seconds[stream].begin()
-        seconds[stream].direct()
+        at, peer = (y, y_peer) if stream % 2 == 0 else (x, x_peer)
+        for k in (2, 1, 3):
+            later.append(
+                push(
+                    summed.at[stream, :, lax.rem(at + k, SIDE)],
+                    got_second.at[stream, k - 1],
+                    q_send.at[stream, k - 1],
+                    q_recv.at[stream, k - 1],
+                    peer(k),
+                )
+            )
+
+    z_copies = []
 
     def last(stream):
-        for h in range(2):
-            total[pl.ds(4 * stream + 2 * h, 2)] = seconds[stream].result(h)
-        for n in range(4 * stream, 4 * stream + 4):
-
-            @pl.when(node != n)
-            def _():
-                push(
-                    total.at[n],
-                    got_z.at[node],
-                    z_send.at[n],
-                    z_recv.at[node],
-                    (rel, n),
+        for k in range(SIDE - 1):
+            arrival(got_second.at[stream, k], q_recv.at[stream, k])
+        value = f32(summed[stream, :, y if stream % 2 == 0 else x])
+        for k in range(SIDE - 1):
+            value = value + f32(got_second[stream, k])
+        total[pl.ds(4 * stream, 4)] = value.astype(jnp.bfloat16)
+        for up in (2 * stream, 2 * stream + 1):
+            cores = (1 - c,) if up == 0 else (0, 1)
+            for number, core in enumerate(cores):
+                z_copies.append(
+                    push(
+                        total.at[2 * up + core],
+                        got_z.at[node],
+                        z_send.at[2 * up + number],
+                        z_recv.at[2 * up + c],
+                        (rel, lax.rem(z + up, 8) * 2 + core),
+                    )
                 )
-
-            @pl.when(node == n)
-            def _():
-                pltpu.make_async_copy(
-                    total.at[n], got_z.at[node], z_recv.at[node]
-                ).start()
-
-    for stream in range(streams):
-        get_d[stream].wait()
-    for ring in firsts[:2]:
-        ring.pass_on()
-    for ring in firsts[2:]:
-        ring.direct()
-    for ring in firsts[2:]:
+        if stream == 0:
+            got_z[node] = total[c]
+
+    for ring in firsts:
         ring.pass_on()
     middle(0)
     middle(1)
-    seconds[0].pass_on()
-    seconds[1].pass_on()
     middle(2)
     middle(3)
     last(0)
     last(1)
-    seconds[2].pass_on()
-    seconds[3].pass_on()
     last(2)
     last(3)
 
@@ -798,16 +745,22 @@
         arrival(got_g.at[m], g_recv.at[m])
     g_out[...] = (got_g[0] + got_g[1]) + (got_g[2] + got_g[3])
 
-    for n in range(NODES):
-        arrival(got_z.at[n], z_recv.at[n])
+    arrival(got_z.at[z * 2 + 1 - c], z_recv.at[1 - c])
+    for up in range(1, 8):
+        for core in range(2):
+            arrival(
+                got_z.at[lax.rem(z + 8 - up, 8) * 2 + core], z_recv.at[2 * up + core]
+            )
     for q in range(4):
         value = own_term[:, q * QUARTER : (q + 1) * QUARTER]
         for step in range(4):
             value = value + f32(got_z[(2 * step + q // 2) * 2 + q % 2])
         d_out[:, q * QUARTER : (q + 1) * QUARTER] = value.astype(jnp.bfloat16)
 
-    for ring in firsts + seconds:
+    for ring in firsts:
         ring.sent()
+    for copy in later + z_copies:
+        copy.wait_send()
     for m in range(4):
         owner = quarter * 4 + m
 
@@ -822,19 +775,6 @@
                 device_id_type=MESH,
             ).wait_send()
 
-    for n in range(NODES):
-
-        @pl.when(node != n)
-        def _():
-            pltpu.make_async_remote_copy(
-                src_ref=total.at[n],
-                dst_ref=got_z.at[node],
-                send_sem=z_send.at[n],
-                recv_sem=z_recv.at[node],
-                device_id=(rel, n),
-                device_id_type=MESH,
-            ).wait_send()
-
 
 def reduce(d_part, g_part, adj, self_weight):
     dma = pltpu.SemaphoreType.DMA
@@ -845,14 +785,12 @@
             jax.ShapeDtypeStruct((2, 32, FEATURE), jnp.float32),
             jax.ShapeDtypeStruct((ROWS, FEATURE), bf16),
         ),
-        in_specs=[ANY, ANY, ANY, ANY],
+        in_specs=[VMEM, VMEM, ANY, ANY],
         out_specs=(VMEM, VMEM),
         scratch_shapes=[
-            pltpu.VMEM((NODES, SIDE, SIDE, ROWS, QUARTER), bf16),
             pltpu.VMEM((4, 6, 2, SIDE, ROWS, QUARTER), bf16),
             pltpu.VMEM((4, 2, 2, SIDE, ROWS, QUARTER), bf16),
-            pltpu.VMEM((4, 6, 2, ROWS, QUARTER), bf16),
-            pltpu.VMEM((4, 2, 2, ROWS, QUARTER), bf16),
+            pltpu.VMEM((4, 3, 4, ROWS, QUARTER), bf16),
             pltpu.VMEM((4, 4, SIDE, ROWS, QUARTER), bf16),
             pltpu.VMEM((NODES, ROWS, QUARTER), bf16),
             pltpu.VMEM((NODES, ROWS, QUARTER), bf16),
@@ -860,9 +798,10 @@
             pltpu.VMEM((ROWS, FEATURE), bf16),
             pltpu.VMEM((FEATURE, FEATURE), bf16),
             dma((2,)),
-            dma((4,)),
-            dma((8, 6)),
-            dma((8, 6)),
+            dma((4, 6)),
+            dma((4, 6)),
+            dma((4, 3)),
+            dma((4, 3)),
             dma((16,)),
             dma((16,)),
             dma((4,)),
@@ -891,21 +830,21 @@
     ) * BLOCKS + tile_target
     meta = jnp.pad(code, ((0, 7), (0, 128 - TILES)))
     adj = out_adjoint[0]
-    tiles, a_rows, x_rows, codes = gather(
-        adj,
-        layer_input.reshape(SIDE, SIDE, ROWS, FEATURE),
-        tile_values[0],
-        meta,
-    )
     stay = functools.partial(
         pltpu.with_memory_space_constraint, memory_space=pltpu.HBM
+    )
+    tiles, a_rows, x_rows, codes = gather(
+        stay(adj),
+        stay(layer_input.reshape(SIDE, SIDE, ROWS, FEATURE)),
+        stay(tile_values[0]),
+        stay(meta),
     )
     d_part, g_part = local(
         stay(codes),
         tile_values[0],
-        stay(tiles.reshape(4 * TILES, EDGE, EDGE)),
-        stay(a_rows.reshape(4 * BLOCKS, EDGE, FEATURE)),
-        stay(x_rows.reshape(NODES * BLOCKS, EDGE, QUARTER)),
+        tiles.reshape(4 * TILES, EDGE, EDGE),
+        a_rows.reshape(4 * BLOCKS, EDGE, FEATURE),
+        x_rows.reshape(NODES * BLOCKS, EDGE, QUARTER),
         stay(rel_weights),
     )
     rel_weight_grad, d_source = reduce(

time: 104 us -> 102 us (0.981)
  Pallas kernels: 101 us -> 97.4 us
    pallas_call x1, Pallas kernels: 13.1 us -> 10.9 us  [local(): pl.pallas_call(local_kernel, out_shape=(jax.ShapeDtypeStruct((buckets, ED...]
where the time goes in v5:
time: 102 us; the launch traced here: 101 us
  Pallas kernels  97.4 us (95%)
  local copies, waits for them, and re-layouts  2.5 us (2%)
    pallas_call x1, Pallas kernels, gather(): pl.pallas_call(gather_kernel, out_shape=(jax.ShapeDtypeStruct((4, TILES,...  49.2 us
    pallas_call x1, Pallas kernels, reduce(): pl.pallas_call(reduce_kernel, out_shape=(jax.ShapeDtypeStruct((2, 32, FEA...  37.3 us
    pallas_call x1, Pallas kernels, local(): pl.pallas_call(local_kernel, out_shape=(jax.ShapeDtypeStruct((buckets, ED...  10.9 us

profile of v5, /device:TPU:1, one launch (start us, length us, event | category | flops | bytes accessed | tf_op | source)
XLA Modules:
  0.0 101.4 jit_solution(9428697940361729306)
XLA Ops:
  0.6 0.0 copy-start
  0.6 0.9 multiply_add_fusion
  1.5 0.6 pad.4.meta
  2.1 49.2 %gather_rows_and_tiles.1 = (bf16[4,64,128,128]{3,2,1,0:T(8,128)(2,1)S(1)}, bf16[4,4,4,64,512]{4,3,2,1,0:T(8,128)(2,1)S(1)}, bf16[16,4,4,64,128]{4,3,2,1,0:T(8,128)(2,1)S(1)}, s32[4,8,128]{2,1,0:T(8,128)S(1)}) custom-call(bf16[64,512]{1,0:T(8,128)(2,1)} %bitcast.22, bf16[4,4,64,512]{3,2,1,0:T(8,128)(2,1)} %bitcast.25, bf16[64,128,128]{2,1,0:T(8,128)(2,1)} %bitcast.17, ...), custom_call_target="tpu_custom_call" | custom-call | bytes 33554432 | tf_op jit(solution)/shard_map/gather_rows_and_tiles/pallas_call | solution.py:377
  51.3 0.0 copy-start.3
  51.3 0.6 copy-done.3
  51.9 0.0 copy-done
  51.9 0.0 copy-start.1
  51.9 0.0 copy-start.2
  51.9 10.9 %tile_products.1 = (bf16[128,128,128]{2,1,0:T(8,128)(2,1)S(1)}, f32[2,128,512]{2,1,0:T(8,128)S(1)}) custom-call(s32[4,8,128]{2,1,0:T(8,128)} %copy-done.3, bf16[64,128,128]{2,1,0:T(8,128)(2,1)S(1)} %bitcast.18, bf16[256,128,128]{2,1,0:T(8,128)(2,1)S(1)} %bitcast.16, bf16[32,128,512]{2,1,0:T(8,128)(2,1)S(1)} %bitcast.20, bf16[128,128,128]{2,1,0:T(8,128)(2,1)S(1)} %bitcast.21, ...), custom_call_target="tpu_custom_call" | custom-call | tf_op jit(solution)/shard_map/tile_products/pallas_call | solution.py:521
  62.8 0.0 copy-done.1
  62.8 0.0 copy-done.2
  62.8 37.3 %sum_terms.1 = (f32[2,32,512]{2,1,0:T(8,128)S(1)}, bf16[64,512]{1,0:T(8,128)(2,1)S(1)}) custom-call(bf16[16,4,4,64,128]{4,3,2,1,0:T(8,128)(2,1)S(1)} %bitcast.19, f32[2,128,512]{2,1,0:T(8,128)S(1)} %get-tuple-element.15.g_part, bf16[64,512]{1,0:T(8,128)(2,1)S(1)} %bitcast.23, bf16[512,512]{1,0:T(8,128)(2,1)S(1)} %copy-done.1), custom_call_target="tpu_custom_call" | custom-call | tf_op jit(solution)/shard_map/sum_terms/pallas_call | solution.py:782
  100.1 0.7 copy.13
  100.8 0.6 copy.14
Async XLA Ops:
  0.6 51.3 %copy-start = (bf16[1,64,128,128]{3,2,1,0:T(8,128)(2,1)S(1)}, bf16[1,64,128,128]{3,2,1,0:T(8,128)(2,1)}, u32[]{:S(2)}) copy-start(bf16[1,64,128,128]{3,2,1,0:T(8,128)(2,1)} %param.13) | copy-start | bytes 6291460
  51.3 0.6 copy-start.3
  51.9 10.9 %copy-start.1 = (bf16[512,512]{1,0:T(8,128)(2,1)S(1)}, bf16[512,512]{1,0:T(8,128)(2,1)}, u32[]{:S(2)}) copy-start(bf16[512,512]{1,0:T(8,128)(2,1)} %self_weight_in.1) | copy-start | bytes 1572868
  51.9 10.9 %copy-start.2 = (bf16[1,64,512]{2,1,0:T(8,128)(2,1)S(1)}, bf16[1,64,512]{2,1,0:T(8,128)(2,1)}, u32[]{:S(2)}) copy-start(bf16[1,64,512]{2,1,0:T(8,128)(2,1)} %param.9) | copy-start | bytes 196612

commit v6 on v5

--- a/solution.py
+++ b/solution.py
@@ -129,6 +129,8 @@
     f_recv,
     a_send,
     a_recv,
+    l_send,
+    l_recv,
     x_send,
     x_recv,
     z_send,
@@ -189,28 +191,24 @@
         shards = (pl.ds(base, cut), pl.ds(base + cut, count - cut))
         return x_all.at[pl.ds(base, count) if h is None else shards[h], px, py]
 
-    def x_ring(stream, leg):
-        number = 2 * stream + leg
-        along_x = (stream + leg) % 2 == 0
-        if along_x:
-            others = y if leg == 0 else every
+    def second_x(stream):
+        if stream % 2 == 1:
             return RingGather(
-                lambda p, h: x_view(stream, p, others, h),
+                lambda p, h: x_view(stream, p, every, h),
                 x,
                 x_peer,
-                x_send.at[number],
-                x_recv.at[number],
-            )
-        others = x if leg == 0 else every
+                x_send.at[stream],
+                x_recv.at[stream],
+            )
         return RingGather(
-            lambda p, h: x_view(stream, others, p, h),
+            lambda p, h: x_view(stream, every, p, h),
             y,
             y_peer,
-            x_send.at[number],
-            x_recv.at[number],
-        )
-
-    x_rings = [[x_ring(stream, leg) for leg in range(2)] for stream in range(4)]
+            x_send.at[stream],
+            x_recv.at[stream],
+        )
+
+    x_rings = [second_x(stream) for stream in range(4)]
 
     greet(x, y, rel, node)
 
@@ -297,11 +295,6 @@
         for ring in a_rings[number]:
             ring.begin()
 
-    for stream in range(4):
-        base, count, _ = streams[stream]
-        for index in range(base, base + count):
-            arrival(x_all.at[index, x, y], z_recv.at[index - 2])
-        x_rings[stream][0].begin()
     t_far = []
     for h in range(2):
         part = pl.ds(h * halves, halves)
@@ -314,19 +307,34 @@
                 (rel, beside * 2 + h),
             )
         )
+    x_first = [[] for _ in streams]
+    for stream in range(4):
+        base, count, _ = streams[stream]
+        for index in range(base, base + count):
+            arrival(x_all.at[index, x, y], z_recv.at[index - 2])
+        mine = x_view(stream, x, y, None)
+        for k in (2, 1, 3):
+            x_first[stream].append(
+                push(
+                    mine,
+                    mine,
+                    l_send.at[stream, k - 1],
+                    l_recv.at[stream, k - 1],
+                    (x_peer if stream % 2 == 0 else y_peer)(k),
+                )
+            )
     for ring in a_rings[0] + a_rings[1]:
         ring.forward()
     for stream in range(4):
-        x_rings[stream][0].forward()
-    for stream in range(4):
-        x_rings[stream][0].finish()
-        x_rings[stream][1].begin()
+        for copy in x_first[stream]:
+            copy.wait_recv()
+        x_rings[stream].begin()
     for ring in a_rings[0] + a_rings[1]:
         ring.finish()
     pair = pl.ds(2 * c, 2)
     a_over = push(a_all.at[pair], a_all.at[pair], s_send.at[1], s_recv.at[1], sibling)
     for stream in range(4):
-        x_rings[stream][1].forward()
+        x_rings[stream].forward()
 
     onward = []
     mine = pl.ds(c * halves, halves)
@@ -342,7 +350,7 @@
             )
         )
     for stream in range(4):
-        x_rings[stream][1].finish()
+        x_rings[stream].finish()
 
     arrival(t_all.at[other], s_recv.at[0])
     arrival(a_all.at[pl.ds(2 - 2 * c, 2)], s_recv.at[1])
@@ -357,9 +365,11 @@
     arrival(x_all.at[1 - c], s_recv.at[4])
     for ring in a_rings[0] + a_rings[1]:
         ring.sent()
-    for rings in x_rings:
-        for ring in rings:
-            ring.sent()
+    for ring in x_rings:
+        ring.sent()
+    for copies in x_first:
+        for copy in copies:
+            copy.wait_send()
     for copy in (
         [a_near, t_near, a_over, x_near]
         + a_first[0]
@@ -380,7 +390,7 @@
             jax.ShapeDtypeStruct((4, TILES, EDGE, EDGE), jnp.bfloat16),
             jax.ShapeDtypeStruct((4, SIDE, SIDE, ROWS, FEATURE), jnp.bfloat16),
             jax.ShapeDtypeStruct((NODES, SIDE, SIDE, ROWS, QUARTER), jnp.bfloat16),
-            jax.ShapeDtypeStruct((4, 8, 128), jnp.int32),
+            jax.ShapeDtypeStruct((4, 8, TILES), jnp.int32),
         ),
         in_specs=[ANY] * 4,
         out_specs=(VMEM, VMEM, VMEM, ANY),
@@ -390,8 +400,10 @@
             dma((2, 2, 3)),
             dma((2, 2, 4)),
             dma((2, 2, 4)),
-            dma((8, 4)),
-            dma((8, 4)),
+            dma((4, 3)),
+            dma((4, 3)),
+            dma((4, 4)),
+            dma((4, 4)),
             dma((14,)),
             dma((14,)),
             dma((3,)),
@@ -524,7 +536,7 @@
             jax.ShapeDtypeStruct((buckets, EDGE, QUARTER), bf16),
             jax.ShapeDtypeStruct((2, QUARTER, FEATURE), jnp.float32),
         ),
-        in_specs=[HBM, VMEM, VMEM, VMEM, VMEM, HBM],
+        in_specs=[ANY, VMEM, VMEM, VMEM, VMEM, HBM],
         out_specs=(VMEM, VMEM),
         scratch_shapes=[
             pltpu.VMEM((2, QUARTER, FEATURE), bf16),
@@ -532,7 +544,7 @@
             pltpu.VMEM((buckets, QUARTER, EDGE), jnp.float32),
             pltpu.VMEM((2, shards * BLOCKS, EDGE, QUARTER), jnp.float32),
             pltpu.VMEM((QUARTER, shards * BLOCKS * EDGE), bf16),
-            pltpu.SMEM((shards, 8, 128), jnp.int32),
+            pltpu.SMEM((shards, 8, TILES), jnp.int32),
             pltpu.SemaphoreType.DMA((2,)),
         ],
         compiler_params=pltpu.CompilerParams(vmem_limit_bytes=24 << 20),
@@ -828,7 +840,7 @@
     code = (
         (tile_dest[:, :, 0] * BLOCKS + tile_src) * 2 + tile_rel
     ) * BLOCKS + tile_target
-    meta = jnp.pad(code, ((0, 7), (0, 128 - TILES)))
+    meta = jnp.broadcast_to(code, (8, TILES))
     adj = out_adjoint[0]
     stay = functools.partial(
         pltpu.with_memory_space_constraint, memory_space=pltpu.HBM
@@ -840,7 +852,7 @@
         stay(meta),
     )
     d_part, g_part = local(
-        stay(codes),
+        codes,
         tile_values[0],
         tiles.reshape(4 * TILES, EDGE, EDGE),
         a_rows.reshape(4 * BLOCKS, EDGE, FEATURE),

time: 102 us -> 100 us (0.980)
    pallas_call x1, Pallas kernels: 49.2 us -> 48.1 us  [gather(): pl.pallas_call(gather_kernel, out_shape=(jax.ShapeDtypeStruct((4, TILES,...]
where the time goes in v6:
time: 100 us; the launch traced here: 99.9 us
  Pallas kernels  96.5 us (96%)
  local copies, waits for them, and re-layouts  1.9 us (2%)
    pallas_call x1, Pallas kernels, gather(): pl.pallas_call(gather_kernel, out_shape=(jax.ShapeDtypeStruct((4, TILES,...  48.1 us
    pallas_call x1, Pallas kernels, reduce(): pl.pallas_call(reduce_kernel, out_shape=(jax.ShapeDtypeStruct((2, 32, FEA...  37.4 us
    pallas_call x1, Pallas kernels, local(): pl.pallas_call(local_kernel, out_shape=(jax.ShapeDtypeStruct((buckets, ED...  10.9 us

profile of v6, /device:TPU:1, one launch (start us, length us, event | category | flops | bytes accessed | tf_op | source)
XLA Modules:
  0.0 99.9 jit_solution(6556698545893243420)
XLA Ops:
  0.6 0.0 copy-start
  0.6 0.9 add_bitcast_fusion
  1.5 0.6 broadcast_in_dim.11.meta
  2.1 48.1 %gather_rows_and_tiles.1 = (bf16[4,64,128,128]{3,2,1,0:T(8,128)(2,1)S(1)}, bf16[4,4,4,64,512]{4,3,2,1,0:T(8,128)(2,1)S(1)}, bf16[16,4,4,64,128]{4,3,2,1,0:T(8,128)(2,1)S(1)}, s32[4,8,64]{2,1,0:T(8,128)S(1)}) custom-call(bf16[64,512]{1,0:T(8,128)(2,1)} %bitcast.24, bf16[4,4,64,512]{3,2,1,0:T(8,128)(2,1)} %bitcast.27, bf16[64,128,128]{2,1,0:T(8,128)(2,1)} %bitcast.19, ...), custom_call_target="tpu_custom_call" | custom-call | bytes 33554432 | tf_op jit(solution)/shard_map/gather_rows_and_tiles/pallas_call | solution.py:387
  50.2 0.0 copy-done
  50.2 0.0 copy-start.1
  50.3 0.0 copy-start.2
  50.3 10.9 %tile_products.1 = (bf16[128,128,128]{2,1,0:T(8,128)(2,1)S(1)}, f32[2,128,512]{2,1,0:T(8,128)S(1)}) custom-call(s32[4,8,64]{2,1,0:T(8,128)S(1)} %get-tuple-element.10.meta_in, bf16[64,128,128]{2,1,0:T(8,128)(2,1)S(1)} %bitcast.20, bf16[256,128,128]{2,1,0:T(8,128)(2,1)S(1)} %bitcast.18, bf16[32,128,512]{2,1,0:T(8,128)(2,1)S(1)} %bitcast.22, ...), custom_call_target="tpu_custom_call" | custom-call | tf_op jit(solution)/shard_map/tile_products/pallas_call | solution.py:533
  61.2 0.0 copy-done.1
  61.2 0.0 copy-done.2
  61.2 37.4 %sum_terms.1 = (f32[2,32,512]{2,1,0:T(8,128)S(1)}, bf16[64,512]{1,0:T(8,128)(2,1)S(1)}) custom-call(bf16[16,4,4,64,128]{4,3,2,1,0:T(8,128)(2,1)S(1)} %bitcast.21, f32[2,128,512]{2,1,0:T(8,128)S(1)} %get-tuple-element.15.g_part, bf16[64,512]{1,0:T(8,128)(2,1)S(1)} %bitcast.25, bf16[512,512]{1,0:T(8,128)(2,1)S(1)} %copy-done.1), custom_call_target="tpu_custom_call" | custom-call | tf_op jit(solution)/shard_map/sum_terms/pallas_call | solution.py:794
  98.6 0.7 copy.13
  99.3 0.6 copy.14
Async XLA Ops:
  0.6 49.6 %copy-start = (bf16[1,64,128,128]{3,2,1,0:T(8,128)(2,1)S(1)}, bf16[1,64,128,128]{3,2,1,0:T(8,128)(2,1)}, u32[]{:S(2)}) copy-start(bf16[1,64,128,128]{3,2,1,0:T(8,128)(2,1)} %param.13) | copy-start | bytes 6291460
  50.2 10.9 %copy-start.1 = (bf16[512,512]{1,0:T(8,128)(2,1)S(1)}, bf16[512,512]{1,0:T(8,128)(2,1)}, u32[]{:S(2)}) copy-start(bf16[512,512]{1,0:T(8,128)(2,1)} %self_weight_in.1) | copy-start | bytes 1572868
  50.3 10.9 %copy-start.2 = (bf16[1,64,512]{2,1,0:T(8,128)(2,1)S(1)}, bf16[1,64,512]{2,1,0:T(8,128)(2,1)}, u32[]{:S(2)}) copy-start(bf16[1,64,512]{2,1,0:T(8,128)(2,1)} %param.9) | copy-start | bytes 196612

commit v7 on v6

--- a/solution.py
+++ b/solution.py
@@ -258,6 +258,18 @@
                 )
             )
 
+    t_far = []
+    for h in range(2):
+        part = pl.ds(h * halves, halves)
+        t_far.append(
+            push(
+                tiles.at[part],
+                t_all.at[away, part],
+                t_send.at[h],
+                t_recv.at[c],
+                (rel, beside * 2 + h),
+            )
+        )
     arrival(a_all.at[near, x, y], t_recv.at[2])
     a_send_first(a_all.at[near, x, y], near, 1)
 
@@ -295,18 +307,6 @@
         for ring in a_rings[number]:
             ring.begin()
 
-    t_far = []
-    for h in range(2):
-        part = pl.ds(h * halves, halves)
-        t_far.append(
-            push(
-                tiles.at[part],
-                t_all.at[away, part],
-                t_send.at[h],
-                t_recv.at[c],
-                (rel, beside * 2 + h),
-            )
-        )
     x_first = [[] for _ in streams]
     for stream in range(4):
         base, count, _ = streams[stream]

time: 100 us -> 98.4 us (0.984)
  Pallas kernels: 96.5 us -> 94.8 us
    pallas_call x1, Pallas kernels: 37.4 us -> 35.8 us  [reduce(): pl.pallas_call(reduce_kernel, out_shape=(jax.ShapeDtypeStruct((2, 32, FEA...]
where the time goes in v7:
time: 98.4 us; the launch traced here: 98.3 us
  Pallas kernels  94.8 us (96%)
  local copies, waits for them, and re-layouts  1.9 us (2%)
    pallas_call x1, Pallas kernels, gather(): pl.pallas_call(gather_kernel, out_shape=(jax.ShapeDtypeStruct((4, TILES,...  48.1 us
    pallas_call x1, Pallas kernels, reduce(): pl.pallas_call(reduce_kernel, out_shape=(jax.ShapeDtypeStruct((2, 32, FEA...  35.8 us
    pallas_call x1, Pallas kernels, local(): pl.pallas_call(local_kernel, out_shape=(jax.ShapeDtypeStruct((buckets, ED...  10.9 us

profile of v7, /device:TPU:1, one launch (start us, length us, event | category | flops | bytes accessed | tf_op | source)
XLA Modules:
  0.0 98.3 jit_solution(4996214145222102509)
XLA Ops:
  0.6 0.0 copy-start
  0.6 0.9 add_bitcast_fusion
  1.5 0.6 broadcast_in_dim.11.meta
  2.1 48.1 %gather_rows_and_tiles.1 = (bf16[4,64,128,128]{3,2,1,0:T(8,128)(2,1)S(1)}, bf16[4,4,4,64,512]{4,3,2,1,0:T(8,128)(2,1)S(1)}, bf16[16,4,4,64,128]{4,3,2,1,0:T(8,128)(2,1)S(1)}, s32[4,8,64]{2,1,0:T(8,128)S(1)}) custom-call(bf16[64,512]{1,0:T(8,128)(2,1)} %bitcast.24, bf16[4,4,64,512]{3,2,1,0:T(8,128)(2,1)} %bitcast.27, bf16[64,128,128]{2,1,0:T(8,128)(2,1)} %bitcast.19, ...), custom_call_target="tpu_custom_call" | custom-call | bytes 33554432 | tf_op jit(solution)/shard_map/gather_rows_and_tiles/pallas_call | solution.py:387
  50.2 0.0 copy-done
  50.2 0.0 copy-start.1
  50.3 0.0 copy-start.2
  50.3 10.9 %tile_products.1 = (bf16[128,128,128]{2,1,0:T(8,128)(2,1)S(1)}, f32[2,128,512]{2,1,0:T(8,128)S(1)}) custom-call(s32[4,8,64]{2,1,0:T(8,128)S(1)} %get-tuple-element.10.meta_in, bf16[64,128,128]{2,1,0:T(8,128)(2,1)S(1)} %bitcast.20, bf16[256,128,128]{2,1,0:T(8,128)(2,1)S(1)} %bitcast.18, bf16[32,128,512]{2,1,0:T(8,128)(2,1)S(1)} %bitcast.22, ...), custom_call_target="tpu_custom_call" | custom-call | tf_op jit(solution)/shard_map/tile_products/pallas_call | solution.py:533
  61.2 0.0 copy-done.1
  61.2 0.0 copy-done.2
  61.2 35.8 %sum_terms.1 = (f32[2,32,512]{2,1,0:T(8,128)S(1)}, bf16[64,512]{1,0:T(8,128)(2,1)S(1)}) custom-call(bf16[16,4,4,64,128]{4,3,2,1,0:T(8,128)(2,1)S(1)} %bitcast.21, f32[2,128,512]{2,1,0:T(8,128)S(1)} %get-tuple-element.15.g_part, bf16[64,512]{1,0:T(8,128)(2,1)S(1)} %bitcast.25, bf16[512,512]{1,0:T(8,128)(2,1)S(1)} %copy-done.1), custom_call_target="tpu_custom_call" | custom-call | tf_op jit(solution)/shard_map/sum_terms/pallas_call | solution.py:794
  97.0 0.7 copy.13
  97.7 0.6 copy.14
Async XLA Ops:
  0.6 49.6 %copy-start = (bf16[1,64,128,128]{3,2,1,0:T(8,128)(2,1)S(1)}, bf16[1,64,128,128]{3,2,1,0:T(8,128)(2,1)}, u32[]{:S(2)}) copy-start(bf16[1,64,128,128]{3,2,1,0:T(8,128)(2,1)} %param.13) | copy-start | bytes 6291460
  50.2 10.9 %copy-start.1 = (bf16[512,512]{1,0:T(8,128)(2,1)S(1)}, bf16[512,512]{1,0:T(8,128)(2,1)}, u32[]{:S(2)}) copy-start(bf16[512,512]{1,0:T(8,128)(2,1)} %self_weight_in.1) | copy-start | bytes 1572868
  50.3 10.9 %copy-start.2 = (bf16[1,64,512]{2,1,0:T(8,128)(2,1)S(1)}, bf16[1,64,512]{2,1,0:T(8,128)(2,1)}, u32[]{:S(2)}) copy-start(bf16[1,64,512]{2,1,0:T(8,128)(2,1)} %param.9) | copy-start | bytes 196612
